TPU v7x, 128 devices: a whole 4x4x4 slice. The times are simulated.
128 devices in a mesh: grp: 4 (over x), row: 32 (over y, z, core).
Axes of the slice: x: 4, y: 4, z: 4, core: 2. Of those that a mesh axis runs over, the one named last changes fastest.
Arguments:
- matrix_tiles: float32 [512, 32, 128, 128], P(('grp', 'row')), may hold values from -2 to 2, as said below
- column_index: int32 [512, 32], P(('grp', 'row')), may hold values from 0 to 511, as said below
- precond: float32 [512, 128, 128], P(('grp', 'row')), may hold values from -12 to 16, as said below
- right_side: float32 [512, 16, 128], P(('grp', 'row')), may hold values from -60 to 60
- lost_group: int32 [1], replicated, may hold values from 0 to 16383
Outputs:
- recovered: float32 [512, 16, 128], P(('grp', 'row'))
- true_residual: float32 [512, 16, 128], P(('grp', 'row'))
Inputs may be any that keep to these rules, and one draw needn't show every extreme that they name: `column_index`: entry 0 of block row i is i; entry 1 is i + 12, or i - 12 where i + 12 passes the end; every entry lies within 12 of its block row. `precond`: every block is symmetric positive definite. `matrix_tiles`: the diagonal tile of each block row is near the identity.
All inputs are finite; a program needn't handle non-finite values.
Results may differ from a plain program's by a relative error of at most 0.0003.
Values sent between devices are 32-bit elements; how exact they have to be, the bound alone decides.
A program may use at most 64 MiB of HBM per device.

v0:
```python
import jax
import jax.numpy as jnp
from jax import lax
from jax.sharding import PartitionSpec as P

REACH = 3
OUTER = 2
INNER = 2
BAND = 12


def from_behind(value, axis, steps):
    count = lax.axis_size(axis)
    first, last = (max(0, -steps), min(count, count - steps))
    return lax.ppermute(value, axis, [(source, source + steps) for source in range(first, last)])


def inner_products(former, latter):
    return jnp.einsum("ica,ida->cd", former, latter, precision=lax.Precision.HIGHEST)


def scaled_by(vector, coeffs):
    return jnp.einsum("ica,cd->ida", vector, coeffs, precision=lax.Precision.HIGHEST)


def solve_sym(matrix, target):
    factor = jnp.linalg.cholesky(0.5 * (matrix + matrix.T))
    middle = lax.linalg.triangular_solve(factor, target, left_side=True, lower=True)
    return lax.linalg.triangular_solve(factor, middle, left_side=True, lower=True, transpose_a=True)


def neighbour(vector, offset):
    return from_behind(vector, ("grp", "row"), offset)


def group_neighbour(vector, offset):
    return from_behind(vector, "row", offset)


def window_of(vector, shifter):
    pieces = [shifter(vector, offset) for offset in range(REACH, 0, -1)]
    pieces.append(vector)
    for offset in range(1, REACH + 1):
        pieces.append(shifter(vector, -offset))
    return jnp.concatenate(pieces, 0)


def tile_product(matrix_tiles, window, local_cols, kept_mask):
    picked = jnp.take(window, local_cols, axis=0)
    if kept_mask is not None:
        picked = picked * kept_mask[:, :, None, None]
    return jnp.einsum("ikab,ikcb->ica", matrix_tiles, picked, precision=lax.Precision.HIGHEST)


def per_device(matrix_tiles, column_index, precond, right_side, lost_group):
    blocks = right_side.shape[0]
    row_count = lax.axis_size("row")
    group_count = lax.axis_size("grp")
    group_blocks = blocks * row_count
    my_group = lax.axis_index("grp")
    my_start = lax.axis_index(("grp", "row")) * blocks
    local_cols = column_index - (my_start - BAND)
    other_mask = (column_index // group_blocks != my_group).astype(jnp.float32)
    own_mask = 1.0 - other_mask
    lost = lost_group[0] % group_count

    def full_product(vector):
        return tile_product(matrix_tiles, window_of(vector, neighbour), local_cols, None)

    solution = jnp.zeros_like(right_side)
    residual = right_side
    direction = right_side
    squares = lax.psum(inner_products(residual, residual), ("grp", "row"))
    for outer_step in range(OUTER):
        applied = full_product(direction)
        curvature = lax.psum(inner_products(direction, applied), ("grp", "row"))
        advance = solve_sym(curvature, squares)
        solution = solution + scaled_by(direction, advance)
        residual = residual - scaled_by(applied, advance)
        squares_next = lax.psum(inner_products(residual, residual), ("grp", "row"))
        mixing = solve_sym(squares, squares_next)
        direction = residual + scaled_by(direction, mixing)
        squares = squares_next
    coupled = tile_product(matrix_tiles, window_of(solution, neighbour), local_cols, other_mask)
    inner_target = right_side - coupled

    def condition(vector):
        return jnp.einsum("iab,icb->ica", precond, vector, precision=lax.Precision.HIGHEST)

    estimate = jnp.zeros_like(inner_target)
    remainder = inner_target
    smoothed = condition(remainder)
    heading = smoothed
    weight = lax.psum(inner_products(remainder, smoothed), "row")
    for inner_step in range(INNER):
        applied = tile_product(
            matrix_tiles, window_of(heading, group_neighbour), local_cols, own_mask
        )
        bending = lax.psum(inner_products(heading, applied), "row")
        advance = solve_sym(bending, weight)
        estimate = estimate + scaled_by(heading, advance)
        remainder = remainder - scaled_by(applied, advance)
        if inner_step + 1 < INNER:
            smoothed = condition(remainder)
            weight_next = lax.psum(inner_products(remainder, smoothed), "row")
            heading = smoothed + scaled_by(heading, solve_sym(weight, weight_next))
            weight = weight_next
    recovered = jnp.where(my_group == lost, estimate, solution)
    true_residual = right_side - full_product(recovered)
    return (recovered, true_residual)


def solution(mesh):
    in_specs = (
        P(("grp", "row"), None, None, None),
        P(("grp", "row"), None),
        P(("grp", "row"), None, None),
        P(("grp", "row"), None, None),
        P(),
    )
    out_specs = (P(("grp", "row"), None, None), P(("grp", "row"), None, None))
    return jax.shard_map(
        per_device, mesh=mesh, in_specs=in_specs, out_specs=out_specs, check_vma=False
    )
```

profile of v0, /device:TPU:1, one launch (start us, length us, event | category | flops | bytes accessed | tf_op | source)
XLA Modules:
  0.0 676.1 jit_solution(15861666429005932232)
XLA Ops:
  0.6 1.4 collective-permute-start.5
  2.1 1.3 collective-permute-start.4
  3.4 3.3 collective-permute-start.3
  6.7 4.2 collective-permute-start.2
  10.9 5.0 collective-permute-start
  17.7 3.0 collective-permute-start.1
  20.7 1.3 collective-permute-done.1
  23.6 9.4 %convolution_bitcast_fusion.9 = f32[4,16,128]{2,1,0:T(8,128)S(1)} fusion(f32[4,32,128,128]{3,2,1,0:T(8,128)} %param.12, f32[4,32,16,128]{3,2,1,0:T(8,128)S(1)} %bitcast.246, pred[4,32]{1,0:T(4,128)(4,1)S(1)} %get-tuple-element.12), kind=kOutput, calls=%fused_computation.26 | convolution fusion | flops 402915328 | bytes 9470080 | tf_op jit(solution)/shard_map/ikab,ikcb->ica/dot_general | solution.py:52
  33.2 79.5 %all-reduce = (f32[16,16]{1,0:T(8,128)S(1)}, f32[16,16]{1,0:T(8,128)S(1)}) all-reduce(f32[16,16]{1,0:T(8,128)S(1)} %convolution_bitcast_fusion.22, f32[16,16]{1,0:T(8,128)S(1)} %convolution_bitcast_fusion.23), channel_id=1, replica_groups=mesh['grp'=4,'row'=32] {'grp','row'}, use_global_device_ids=true, to_apply=%region_3.6 | all-reduce | flops 512 | bytes 4096 | tf_op jit(solution)/shard_map/psum | solution.py:73
  112.9 1.5 cholesky.115
  115.7 1.2 custom-call.21
  117.0 1.5 cholesky.104
  119.8 1.2 custom-call.19
  121.8 62.5 %psum.58 = f32[16,16]{1,0:T(8,128)S(1)} all-reduce(f32[16,16]{1,0:T(8,128)S(1)} %convolution_bitcast_fusion.20), channel_id=1, replica_groups=mesh['grp'=4,'row'=32] {'grp','row'}, use_global_device_ids=true, to_apply=%region_4.9 | all-reduce | flops 256 | bytes 2048 | tf_op jit(solution)/shard_map/psum | solution.py:80
  184.9 3.9 collective-permute-start.6
  188.9 1.3 collective-permute-start.11
  190.2 1.3 collective-permute-start.10
  191.5 1.9 collective-permute-start.9
  193.4 3.6 collective-permute-start.8
  197.1 4.6 collective-permute-start.7
  201.7 1.0 collective-permute-done.7
  203.6 9.4 %convolution_bitcast_fusion.6 = f32[4,16,128]{2,1,0:T(8,128)S(1)} fusion(f32[4,32,128,128]{3,2,1,0:T(8,128)} %param.12, f32[4,32,16,128]{3,2,1,0:T(8,128)S(1)} %bitcast.247, pred[4,32]{1,0:T(4,128)(4,1)S(1)} %get-tuple-element.12), kind=kOutput, calls=%fused_computation.21 | convolution fusion | flops 402915328 | bytes 9470080 | tf_op jit(solution)/shard_map/ikab,ikcb->ica/dot_general | solution.py:52
  213.1 73.5 %psum.59 = f32[16,16]{1,0:T(8,128)S(1)} all-reduce(f32[16,16]{1,0:T(8,128)S(1)} %convolution_bitcast_fusion.18), channel_id=1, replica_groups=mesh['grp'=4,'row'=32] {'grp','row'}, use_global_device_ids=true, to_apply=%region_5.10 | all-reduce | flops 256 | bytes 2048 | tf_op jit(solution)/shard_map/psum | solution.py:76
  286.8 1.5 cholesky.126
  289.5 1.2 custom-call.23
  291.4 4.0 collective-permute-start.12
  296.0 1.3 collective-permute-start.17
  297.3 1.3 collective-permute-start.16
  298.6 1.9 collective-permute-start.15
  300.6 3.6 collective-permute-start.14
  304.2 4.3 collective-permute-start.13
  308.6 1.0 collective-permute-done.13
  310.4 9.4 %fusion.5 = f32[4,16,128]{2,1,0:T(8,128)S(1)} fusion(f32[4,16,128]{2,1,0:T(8,128)S(1)} %copy-done.1, f32[4,32,128,128]{3,2,1,0:T(8,128)} %param.12, f32[4,32,16,128]{3,2,1,0:T(8,128)S(1)} %bitcast.242, f32[4,32]{1,0:T(4,128)S(1)} %get-tuple-element.11, pred[4,32]{1,0:T(4,128)(4,1)S(1)} %get-tuple-element.12), kind=kOutput, calls=%fused_computation.18 | convolution fusion | flops 403185664 | bytes 9503360 | tf_op jit(solution)/shard_map/ikab,ikcb->ica/dot_general | solution.py:52
  320.4 5.6 collective-permute-start.18
  326.2 1.3 collective-permute-start.23
  327.5 1.3 collective-permute-start.22
  328.8 1.9 collective-permute-start.21
  330.7 3.6 collective-permute-start.20
  334.4 4.3 collective-permute-start.19
  338.7 1.0 collective-permute-done.19
  340.6 9.4 %convolution_bitcast_fusion.4 = f32[4,16,128]{2,1,0:T(8,128)S(1)} fusion(f32[4,32,128,128]{3,2,1,0:T(8,128)} %param.12, f32[4,32,16,128]{3,2,1,0:T(8,128)S(1)} %bitcast.243, f32[4,32]{1,0:T(4,128)S(1)} %get-tuple-element.10, pred[4,32]{1,0:T(4,128)(4,1)S(1)} %get-tuple-element.12), kind=kOutput, calls=%fused_computation.16 | convolution fusion | flops 403177472 | bytes 9470592 | tf_op jit(solution)/shard_map/ikab,ikcb->ica/dot_general | solution.py:52
  350.1 125.0 %all-reduce.1 = (f32[16,16]{1,0:T(8,128)S(1)}, f32[16,16]{1,0:T(8,128)S(1)}) all-reduce(f32[16,16]{1,0:T(8,128)S(1)} %convolution_bitcast_fusion.15, f32[16,16]{1,0:T(8,128)S(1)} %convolution_bitcast_fusion.16), channel_id=1, replica_groups=mesh['grp'=4,'row'=32] {'row'}, use_global_device_ids=true, to_apply=%region_7.12 | all-reduce | flops 512 | bytes 4096 | tf_op jit(solution)/shard_map/psum | solution.py:94
  475.3 1.5 cholesky.137
  478.1 1.2 custom-call.25
  480.1 1.5 cholesky.148
  482.9 1.2 custom-call.27
  484.8 68.7 %psum.62 = f32[16,16]{1,0:T(8,128)S(1)} all-reduce(f32[16,16]{1,0:T(8,128)S(1)} %convolution_bitcast_fusion.13), channel_id=1, replica_groups=mesh['grp'=4,'row'=32] {'row'}, use_global_device_ids=true, to_apply=%region_8.13 | all-reduce | flops 256 | bytes 2048 | tf_op jit(solution)/shard_map/psum | solution.py:105
  554.0 1.3 collective-permute-start.24
  555.5 1.3 collective-permute-start.29
  556.8 1.3 collective-permute-start.28
  558.1 2.6 collective-permute-start.27
  560.7 4.2 collective-permute-start.26
  564.9 4.2 collective-permute-start.25
  570.7 9.4 %convolution_bitcast_fusion.1 = f32[4,16,128]{2,1,0:T(8,128)S(1)} fusion(f32[4,32,128,128]{3,2,1,0:T(8,128)} %param.12, f32[4,32,16,128]{3,2,1,0:T(8,128)S(1)} %bitcast.244, f32[4,32]{1,0:T(4,128)S(1)} %get-tuple-element.10, pred[4,32]{1,0:T(4,128)(4,1)S(1)} %get-tuple-element.12), kind=kOutput, calls=%fused_computation.11 | convolution fusion | flops 403177472 | bytes 9470592 | tf_op jit(solution)/shard_map/ikab,ikcb->ica/dot_general | solution.py:52
  580.3 62.6 %psum.63 = f32[16,16]{1,0:T(8,128)S(1)} all-reduce(f32[16,16]{1,0:T(8,128)S(1)} %convolution_bitcast_fusion.11), channel_id=1, replica_groups=mesh['grp'=4,'row'=32] {'row'}, use_global_device_ids=true, to_apply=%region_9.14 | all-reduce | flops 256 | bytes 2048 | tf_op jit(solution)/shard_map/psum | solution.py:99
  643.1 1.5 cholesky.159
  645.9 1.2 custom-call.29
  647.7 1.3 collective-permute-start.30
  649.0 1.3 collective-permute-start.35
  650.3 1.3 collective-permute-start.34
  651.6 4.4 collective-permute-start.33
  656.0 4.2 collective-permute-start.32
  660.2 4.0 collective-permute-start.31
  666.1 10.0 %fusion = f32[4,16,128]{2,1,0:T(8,128)} fusion(f32[4,16,128]{2,1,0:T(8,128)S(1)} %copy-done.1, f32[4,32,128,128]{3,2,1,0:T(8,128)} %param.12, f32[4,32,16,128]{3,2,1,0:T(8,128)S(1)} %bitcast.245, pred[4,32]{1,0:T(4,128)(4,1)S(1)} %get-tuple-element.12), kind=kOutput, calls=%fused_computation.7 | convolution fusion | flops 402923520 | bytes 9502848 | tf_op jit(solution)/shard_map/ikab,ikcb->ica/dot_general | solution.py:52
  (163 shorter events, 23.9 us)
Async XLA Ops:
  0.6 319.2 %copy-start = (f32[4,128,128]{2,1,0:T(8,128)S(1)}, f32[4,128,128]{2,1,0:T(8,128)}, u32[]{:S(2)}) copy-start(f32[4,128,128]{2,1,0:T(8,128)} %param.14) | copy-start | bytes 786436
  0.6 22.2 %collective-permute-start.5 = (f32[4,16,128]{2,1,0:T(8,128)}, f32[4,16,128]{2,1,0:T(8,128)S(1)}, u32[]{:S(2)}, u32[]{:S(2)}) collective-permute-start(f32[4,16,128]{2,1,0:T(8,128)} %param.15), channel_id=1, source_target_pairs={{3,0},{4,1},{5,2},{6,3},{7,4},{8,5},{9,6},{10,7},{11,8},{12,9},{13... | collective-permute-start | bytes 98312 | tf_op jit(solution)/shard_map/ppermute | solution.py:15
  2.1 20.7 %collective-permute-start.4 = (f32[4,16,128]{2,1,0:T(8,128)}, f32[4,16,128]{2,1,0:T(8,128)S(1)}, u32[]{:S(2)}, u32[]{:S(2)}) collective-permute-start(f32[4,16,128]{2,1,0:T(8,128)} %param.15), channel_id=1, source_target_pairs={{2,0},{3,1},{4,2},{5,3},{6,4},{7,5},{8,6},{9,7},{10,8},{11,9},{12,... | collective-permute-start | bytes 98312 | tf_op jit(solution)/shard_map/ppermute | solution.py:15
  3.4 19.4 %collective-permute-start.3 = (f32[4,16,128]{2,1,0:T(8,128)}, f32[4,16,128]{2,1,0:T(8,128)S(1)}, u32[]{:S(2)}, u32[]{:S(2)}) collective-permute-start(f32[4,16,128]{2,1,0:T(8,128)} %param.15), channel_id=1, source_target_pairs={{1,0},{2,1},{3,2},{4,3},{5,4},{6,5},{7,6},{8,7},{9,8},{10,9},{11,1... | collective-permute-start | bytes 98312 | tf_op jit(solution)/shard_map/ppermute | solution.py:15
  6.7 15.3 %collective-permute-start.2 = (f32[4,16,128]{2,1,0:T(8,128)}, f32[4,16,128]{2,1,0:T(8,128)S(1)}, u32[]{:S(2)}, u32[]{:S(2)}) collective-permute-start(f32[4,16,128]{2,1,0:T(8,128)} %param.15), channel_id=1, source_target_pairs={{0,1},{1,2},{2,3},{3,4},{4,5},{5,6},{6,7},{7,8},{8,9},{9,10},{10,1... | collective-permute-start | bytes 98312 | tf_op jit(solution)/shard_map/ppermute | solution.py:15
  10.9 6.7 collective-permute-start
  16.8 16.2 %copy-start.1 = (f32[4,16,128]{2,1,0:T(8,128)S(1)}, f32[4,16,128]{2,1,0:T(8,128)}, u32[]{:S(2)}) copy-start(f32[4,16,128]{2,1,0:T(8,128)} %param.15) | copy-start | bytes 98308
  17.7 4.4 collective-permute-start.1
  184.9 12.2 %collective-permute-start.6 = (f32[4,16,128]{2,1,0:T(8,128)S(1)}, f32[4,16,128]{2,1,0:T(8,128)S(1)}, u32[]{:S(2)}, u32[]{:S(2)}) collective-permute-start(f32[4,16,128]{2,1,0:T(8,128)S(1)} %fusion.7), channel_id=1, source_target_pairs={{0,3},{1,4},{2,5},{3,6},{4,7},{5,8},{6,9},{7,10},{8,11},{9,12},{10... | collective-permute-start | bytes 98312 | tf_op jit(solution)/shard_map/ppermute | solution.py:15
  188.9 13.9 %collective-permute-start.11 = (f32[4,16,128]{2,1,0:T(8,128)S(1)}, f32[4,16,128]{2,1,0:T(8,128)S(1)}, u32[]{:S(2)}, u32[]{:S(2)}) collective-permute-start(f32[4,16,128]{2,1,0:T(8,128)S(1)} %fusion.7), channel_id=1, source_target_pairs={{3,0},{4,1},{5,2},{6,3},{7,4},{8,5},{9,6},{10,7},{11,8},{12,9},{13... | collective-permute-start | bytes 98312 | tf_op jit(solution)/shard_map/ppermute | solution.py:15
  190.2 12.6 %collective-permute-start.10 = (f32[4,16,128]{2,1,0:T(8,128)S(1)}, f32[4,16,128]{2,1,0:T(8,128)S(1)}, u32[]{:S(2)}, u32[]{:S(2)}) collective-permute-start(f32[4,16,128]{2,1,0:T(8,128)S(1)} %fusion.7), channel_id=1, source_target_pairs={{2,0},{3,1},{4,2},{5,3},{6,4},{7,5},{8,6},{9,7},{10,8},{11,9},{12,... | collective-permute-start | bytes 98312 | tf_op jit(solution)/shard_map/ppermute | solution.py:15
  191.5 11.2 %collective-permute-start.9 = (f32[4,16,128]{2,1,0:T(8,128)S(1)}, f32[4,16,128]{2,1,0:T(8,128)S(1)}, u32[]{:S(2)}, u32[]{:S(2)}) collective-permute-start(f32[4,16,128]{2,1,0:T(8,128)S(1)} %fusion.7), channel_id=1, source_target_pairs={{1,0},{2,1},{3,2},{4,3},{5,4},{6,5},{7,6},{8,7},{9,8},{10,9},{11,1... | collective-permute-start | bytes 98312 | tf_op jit(solution)/shard_map/ppermute | solution.py:15
  193.4 9.3 %collective-permute-start.8 = (f32[4,16,128]{2,1,0:T(8,128)S(1)}, f32[4,16,128]{2,1,0:T(8,128)S(1)}, u32[]{:S(2)}, u32[]{:S(2)}) collective-permute-start(f32[4,16,128]{2,1,0:T(8,128)S(1)} %fusion.7), channel_id=1, source_target_pairs={{0,1},{1,2},{2,3},{3,4},{4,5},{5,6},{6,7},{7,8},{8,9},{9,10},{10,1... | collective-permute-start | bytes 98312 | tf_op jit(solution)/shard_map/ppermute | solution.py:15
  197.1 5.6 collective-permute-start.7
  202.7 92.6 %copy-start.3 = (s32[4,32]{1,0:T(4,128)S(1)}, s32[4,32]{1,0:T(4,128)}, u32[]{:S(2)}) copy-start(s32[4,32]{1,0:T(4,128)} %param.13) | copy-start | bytes 1540
  291.4 12.8 %collective-permute-start.12 = (f32[4,16,128]{2,1,0:T(8,128)S(1)}, f32[4,16,128]{2,1,0:T(8,128)S(1)}, u32[]{:S(2)}, u32[]{:S(2)}) collective-permute-start(f32[4,16,128]{2,1,0:T(8,128)S(1)} %fusion.6), channel_id=1, source_target_pairs={{0,3},{1,4},{2,5},{3,6},{4,7},{5,8},{6,9},{7,10},{8,11},{9,12},{10... | collective-permute-start | bytes 98312 | tf_op jit(solution)/shard_map/ppermute | solution.py:15
  296.0 13.6 %collective-permute-start.17 = (f32[4,16,128]{2,1,0:T(8,128)S(1)}, f32[4,16,128]{2,1,0:T(8,128)S(1)}, u32[]{:S(2)}, u32[]{:S(2)}) collective-permute-start(f32[4,16,128]{2,1,0:T(8,128)S(1)} %fusion.6), channel_id=1, source_target_pairs={{3,0},{4,1},{5,2},{6,3},{7,4},{8,5},{9,6},{10,7},{11,8},{12,9},{13... | collective-permute-start | bytes 98312 | tf_op jit(solution)/shard_map/ppermute | solution.py:15
  297.3 12.3 %collective-permute-start.16 = (f32[4,16,128]{2,1,0:T(8,128)S(1)}, f32[4,16,128]{2,1,0:T(8,128)S(1)}, u32[]{:S(2)}, u32[]{:S(2)}) collective-permute-start(f32[4,16,128]{2,1,0:T(8,128)S(1)} %fusion.6), channel_id=1, source_target_pairs={{2,0},{3,1},{4,2},{5,3},{6,4},{7,5},{8,6},{9,7},{10,8},{11,9},{12,... | collective-permute-start | bytes 98312 | tf_op jit(solution)/shard_map/ppermute | solution.py:15
  298.6 11.0 %collective-permute-start.15 = (f32[4,16,128]{2,1,0:T(8,128)S(1)}, f32[4,16,128]{2,1,0:T(8,128)S(1)}, u32[]{:S(2)}, u32[]{:S(2)}) collective-permute-start(f32[4,16,128]{2,1,0:T(8,128)S(1)} %fusion.6), channel_id=1, source_target_pairs={{1,0},{2,1},{3,2},{4,3},{5,4},{6,5},{7,6},{8,7},{9,8},{10,9},{11,1... | collective-permute-start | bytes 98312 | tf_op jit(solution)/shard_map/ppermute | solution.py:15
  300.6 9.0 %collective-permute-start.14 = (f32[4,16,128]{2,1,0:T(8,128)S(1)}, f32[4,16,128]{2,1,0:T(8,128)S(1)}, u32[]{:S(2)}, u32[]{:S(2)}) collective-permute-start(f32[4,16,128]{2,1,0:T(8,128)S(1)} %fusion.6), channel_id=1, source_target_pairs={{0,1},{1,2},{2,3},{3,4},{4,5},{5,6},{6,7},{7,8},{8,9},{9,10},{10,1... | collective-permute-start | bytes 98312 | tf_op jit(solution)/shard_map/ppermute | solution.py:15
  304.2 5.4 collective-permute-start.13
  320.4 14.0 %collective-permute-start.18 = (f32[4,16,128]{2,1,0:T(8,128)S(1)}, f32[4,16,128]{2,1,0:T(8,128)S(1)}, u32[]{:S(2)}, u32[]{:S(2)}) collective-permute-start(f32[4,16,128]{2,1,0:T(8,128)S(1)} %fusion.81), channel_id=1, source_target_pairs={{0,3},{1,4},{2,5},{3,6},{4,7},{5,8},{6,9},{7,10},{8,11},{9,12},{10... | collective-permute-start | bytes 98312 | tf_op jit(solution)/shard_map/ppermute | solution.py:15
  326.2 13.6 %collective-permute-start.23 = (f32[4,16,128]{2,1,0:T(8,128)S(1)}, f32[4,16,128]{2,1,0:T(8,128)S(1)}, u32[]{:S(2)}, u32[]{:S(2)}) collective-permute-start(f32[4,16,128]{2,1,0:T(8,128)S(1)} %fusion.81), channel_id=1, source_target_pairs={{3,0},{4,1},{5,2},{6,3},{7,4},{8,5},{9,6},{10,7},{11,8},{12,9},{13... | collective-permute-start | bytes 98312 | tf_op jit(solution)/shard_map/ppermute | solution.py:15
  327.5 12.3 %collective-permute-start.22 = (f32[4,16,128]{2,1,0:T(8,128)S(1)}, f32[4,16,128]{2,1,0:T(8,128)S(1)}, u32[]{:S(2)}, u32[]{:S(2)}) collective-permute-start(f32[4,16,128]{2,1,0:T(8,128)S(1)} %fusion.81), channel_id=1, source_target_pairs={{2,0},{3,1},{4,2},{5,3},{6,4},{7,5},{8,6},{9,7},{10,8},{11,9},{12,... | collective-permute-start | bytes 98312 | tf_op jit(solution)/shard_map/ppermute | solution.py:15
  328.8 11.0 %collective-permute-start.21 = (f32[4,16,128]{2,1,0:T(8,128)S(1)}, f32[4,16,128]{2,1,0:T(8,128)S(1)}, u32[]{:S(2)}, u32[]{:S(2)}) collective-permute-start(f32[4,16,128]{2,1,0:T(8,128)S(1)} %fusion.81), channel_id=1, source_target_pairs={{1,0},{2,1},{3,2},{4,3},{5,4},{6,5},{7,6},{8,7},{9,8},{10,9},{11,1... | collective-permute-start | bytes 98312 | tf_op jit(solution)/shard_map/ppermute | solution.py:15
  330.7 9.0 %collective-permute-start.20 = (f32[4,16,128]{2,1,0:T(8,128)S(1)}, f32[4,16,128]{2,1,0:T(8,128)S(1)}, u32[]{:S(2)}, u32[]{:S(2)}) collective-permute-start(f32[4,16,128]{2,1,0:T(8,128)S(1)} %fusion.81), channel_id=1, source_target_pairs={{0,1},{1,2},{2,3},{3,4},{4,5},{5,6},{6,7},{7,8},{8,9},{9,10},{10,1... | collective-permute-start | bytes 98312 | tf_op jit(solution)/shard_map/ppermute | solution.py:15
  334.4 5.4 collective-permute-start.19
  554.0 10.8 %collective-permute-start.24 = (f32[4,16,128]{2,1,0:T(8,128)S(1)}, f32[4,16,128]{2,1,0:T(8,128)S(1)}, u32[]{:S(2)}, u32[]{:S(2)}) collective-permute-start(f32[4,16,128]{2,1,0:T(8,128)S(1)} %fusion.3), channel_id=1, source_target_pairs={{0,3},{1,4},{2,5},{3,6},{4,7},{5,8},{6,9},{7,10},{8,11},{9,12},{10... | collective-permute-start | bytes 98312 | tf_op jit(solution)/shard_map/ppermute | solution.py:15
  555.5 14.5 %collective-permute-start.29 = (f32[4,16,128]{2,1,0:T(8,128)S(1)}, f32[4,16,128]{2,1,0:T(8,128)S(1)}, u32[]{:S(2)}, u32[]{:S(2)}) collective-permute-start(f32[4,16,128]{2,1,0:T(8,128)S(1)} %fusion.3), channel_id=1, source_target_pairs={{3,0},{4,1},{5,2},{6,3},{7,4},{8,5},{9,6},{10,7},{11,8},{12,9},{13... | collective-permute-start | bytes 98312 | tf_op jit(solution)/shard_map/ppermute | solution.py:15
  556.8 13.1 %collective-permute-start.28 = (f32[4,16,128]{2,1,0:T(8,128)S(1)}, f32[4,16,128]{2,1,0:T(8,128)S(1)}, u32[]{:S(2)}, u32[]{:S(2)}) collective-permute-start(f32[4,16,128]{2,1,0:T(8,128)S(1)} %fusion.3), channel_id=1, source_target_pairs={{2,0},{3,1},{4,2},{5,3},{6,4},{7,5},{8,6},{9,7},{10,8},{11,9},{12,... | collective-permute-start | bytes 98312 | tf_op jit(solution)/shard_map/ppermute | solution.py:15
  558.1 11.8 %collective-permute-start.27 = (f32[4,16,128]{2,1,0:T(8,128)S(1)}, f32[4,16,128]{2,1,0:T(8,128)S(1)}, u32[]{:S(2)}, u32[]{:S(2)}) collective-permute-start(f32[4,16,128]{2,1,0:T(8,128)S(1)} %fusion.3), channel_id=1, source_target_pairs={{1,0},{2,1},{3,2},{4,3},{5,4},{6,5},{7,6},{8,7},{9,8},{10,9},{11,1... | collective-permute-start | bytes 98312 | tf_op jit(solution)/shard_map/ppermute | solution.py:15
  560.7 9.2 %collective-permute-start.26 = (f32[4,16,128]{2,1,0:T(8,128)S(1)}, f32[4,16,128]{2,1,0:T(8,128)S(1)}, u32[]{:S(2)}, u32[]{:S(2)}) collective-permute-start(f32[4,16,128]{2,1,0:T(8,128)S(1)} %fusion.3), channel_id=1, source_target_pairs={{0,1},{1,2},{2,3},{3,4},{4,5},{5,6},{6,7},{7,8},{8,9},{9,10},{10,1... | collective-permute-start | bytes 98312 | tf_op jit(solution)/shard_map/ppermute | solution.py:15
  564.9 5.0 collective-permute-start.25
  647.7 28.3 %copy-start.2 = (f32[4,16,128]{2,1,0:T(8,128)}, f32[4,16,128]{2,1,0:T(8,128)S(1)}, u32[]{:S(2)}) copy-start(f32[4,16,128]{2,1,0:T(8,128)S(1)} %fusion.2) | copy-start | bytes 98308
  647.7 12.4 %collective-permute-start.30 = (f32[4,16,128]{2,1,0:T(8,128)S(1)}, f32[4,16,128]{2,1,0:T(8,128)S(1)}, u32[]{:S(2)}, u32[]{:S(2)}) collective-permute-start(f32[4,16,128]{2,1,0:T(8,128)S(1)} %fusion.2), channel_id=1, source_target_pairs={{0,3},{1,4},{2,5},{3,6},{4,7},{5,8},{6,9},{7,10},{8,11},{9,12},{10... | collective-permute-start | bytes 98312 | tf_op jit(solution)/shard_map/ppermute | solution.py:15
  649.0 16.2 %collective-permute-start.35 = (f32[4,16,128]{2,1,0:T(8,128)S(1)}, f32[4,16,128]{2,1,0:T(8,128)S(1)}, u32[]{:S(2)}, u32[]{:S(2)}) collective-permute-start(f32[4,16,128]{2,1,0:T(8,128)S(1)} %fusion.2), channel_id=1, source_target_pairs={{3,0},{4,1},{5,2},{6,3},{7,4},{8,5},{9,6},{10,7},{11,8},{12,9},{13... | collective-permute-start | bytes 98312 | tf_op jit(solution)/shard_map/ppermute | solution.py:15
  650.3 14.9 %collective-permute-start.34 = (f32[4,16,128]{2,1,0:T(8,128)S(1)}, f32[4,16,128]{2,1,0:T(8,128)S(1)}, u32[]{:S(2)}, u32[]{:S(2)}) collective-permute-start(f32[4,16,128]{2,1,0:T(8,128)S(1)} %fusion.2), channel_id=1, source_target_pairs={{2,0},{3,1},{4,2},{5,3},{6,4},{7,5},{8,6},{9,7},{10,8},{11,9},{12,... | collective-permute-start | bytes 98312 | tf_op jit(solution)/shard_map/ppermute | solution.py:15
  651.6 13.6 %collective-permute-start.33 = (f32[4,16,128]{2,1,0:T(8,128)S(1)}, f32[4,16,128]{2,1,0:T(8,128)S(1)}, u32[]{:S(2)}, u32[]{:S(2)}) collective-permute-start(f32[4,16,128]{2,1,0:T(8,128)S(1)} %fusion.2), channel_id=1, source_target_pairs={{1,0},{2,1},{3,2},{4,3},{5,4},{6,5},{7,6},{8,7},{9,8},{10,9},{11,1... | collective-permute-start | bytes 98312 | tf_op jit(solution)/shard_map/ppermute | solution.py:15
  656.0 9.2 %collective-permute-start.32 = (f32[4,16,128]{2,1,0:T(8,128)S(1)}, f32[4,16,128]{2,1,0:T(8,128)S(1)}, u32[]{:S(2)}, u32[]{:S(2)}) collective-permute-start(f32[4,16,128]{2,1,0:T(8,128)S(1)} %fusion.2), channel_id=1, source_target_pairs={{0,1},{1,2},{2,3},{3,4},{4,5},{5,6},{6,7},{7,8},{8,9},{9,10},{10,1... | collective-permute-start | bytes 98312 | tf_op jit(solution)/shard_map/ppermute | solution.py:15
  660.2 5.0 collective-permute-start.31
where the time goes:
time: 687 us; the launch traced here: 676 us
  blocking collectives  472 us (69%)
  starting transfers between devices  101 us (15%)
  matrix products  63.8 us (9%)
  other arithmetic  24.9 us (4%)
    psum x1, blocking collectives, per_device(): weight = lax.psum(inner_products(remainder, smoothed), 'row')  125 us
    ppermute x36, starting transfers between devices, from_behind(): lax.ppermute(value, axis, [(source, source + steps) for source in range(f...  101 us
    psum x1, blocking collectives, per_device(): squares = lax.psum(inner_products(residual, residual), ('grp', 'row'))  79.5 us
    psum x1, blocking collectives, per_device(): curvature = lax.psum(inner_products(direction, applied), ('grp', 'row'))  73.5 us
    psum x1, blocking collectives, per_device(): weight_next = lax.psum(inner_products(remainder, smoothed), 'row')  68.7 us
    psum x1, blocking collectives, per_device(): bending = lax.psum(inner_products(heading, applied), 'row')  62.6 us
    psum x1, blocking collectives, per_device(): squares_next = lax.psum(inner_products(residual, residual), ('grp', 'row'))  62.5 us
    dot_general x6, matrix products, tile_product(): jnp.einsum('ikab,ikcb->ica', matrix_tiles, picked, precision=lax.Precisio...  57 us
  transfers between devices with their start and end apart: 36, of which 6 were waited for; matrix products, arithmetic and copies ran while one was open for 0% of the time, Pallas kernels for 0%

commit v1 on v0

v1 whole, which is shorter than its diff:
```python
import functools

import jax
import jax.numpy as jnp
from jax import lax
from jax.experimental import pallas as pl
from jax.experimental.pallas import tpu as pltpu
from jax.sharding import PartitionSpec as P

BAND = 12
F32 = jnp.float32
BF16 = jnp.bfloat16
MESH = pl.DeviceIdType.MESH
N_GRP, N_ROW, BR, K, COLS, TB = 4, 32, 4, 32, 16, 128
REACH = 3
WIN = BR * (2 * REACH + 1)
CELL = 8
FAR = (N_GRP * N_ROW) // CELL


def mm(a, b, ca=1, cb=0):
    return lax.dot_general(
        a, b, (((ca,), (cb,)), ((), ())), precision=lax.Precision.HIGHEST, preferred_element_type=F32
    )


def split(x):
    hi = x.astype(BF16)
    return hi, (x - hi.astype(F32)).astype(BF16)


def eye16():
    r = lax.broadcasted_iota(jnp.int32, (COLS, COLS), 0)
    c = lax.broadcasted_iota(jnp.int32, (COLS, COLS), 1)
    return (r == c).astype(F32)


def sym(g):
    return 0.5 * (g + g.T)


def eliminate(*systems):
    mats = [jnp.concatenate([s, h], axis=1) for s, h in systems]
    rows = lax.broadcasted_iota(jnp.int32, mats[0].shape, 0)
    for j in range(COLS):
        for n, m in enumerate(mats):
            row = m[j : j + 1, :] / m[j : j + 1, j : j + 1]
            mats[n] = jnp.where(rows == j, row, m - m[:, j : j + 1] * row)
    return [m[:, COLS:] for m in mats]


def flat(v):
    return jnp.concatenate([v[i] for i in range(BR)], axis=1)


def kernel(
    cols_ref, lost_ref, tiles_ref, pre_ref, b_ref, rec_ref, tres_ref,
    stage, zstage, hl, zhl, win, winb, rhs, msg, near, far0, far1, far2, far3, local,
    load_sem, hs_sem, hr_sem, ns_sem, nr_sem, fs_sem, fr_sem,
):
    g = lax.axis_index("grp")
    r = lax.axis_index("row")
    d = g * N_ROW + r
    cell = r // CELL
    pos = lax.rem(r, CELL)
    my_far = g * (N_ROW // CELL) + cell
    first = d * BR - BAND

    def near_dev(n):
        return (g, cell * CELL + lax.rem(pos + n, CELL))

    def far_dev(n):
        f = lax.rem(my_far + n, FAR)
        return (f // (N_ROW // CELL), lax.rem(f, N_ROW // CELL) * CELL + pos)

    def halo_dev(o):
        t = lax.rem(d + o + N_GRP * N_ROW, N_GRP * N_ROW)
        return (t // N_ROW, lax.rem(t, N_ROW))

    offsets = [1, -1, 2, -2, 3, -3]
    fars = [far0, far1, far2, far3]

    for i in range(BR):
        pltpu.make_async_copy(tiles_ref.at[i], stage.at[i], load_sem.at[i]).start()
    pltpu.make_async_copy(pre_ref, zstage, load_sem.at[BR]).start()

    barrier = pltpu.get_barrier_semaphore()
    for o in offsets:
        pl.semaphore_signal(barrier, inc=1, device_id=halo_dev(o), device_id_type=MESH)
    for n in range(1, CELL):
        pl.semaphore_signal(barrier, inc=1, device_id=near_dev(n), device_id_type=MESH)
    for n in range(1, FAR):
        pl.semaphore_signal(barrier, inc=1, device_id=far_dev(n), device_id_type=MESH)
    win[0, BAND : BAND + BR] = b_ref[...]

    def localise(k, carry):
        for i in range(BR):
            local[i, k] = jnp.clip(cols_ref[i, k] - first, 0, WIN - 1)
        return carry

    lax.fori_loop(0, K, localise, 0)
    pl.semaphore_wait(barrier, len(offsets) + CELL - 1 + FAR - 1)

    def halo_send(rd):
        for o in offsets:
            pltpu.make_async_remote_copy(
                src_ref=win.at[rd, pl.ds(BAND, BR)],
                dst_ref=win.at[rd, pl.ds((REACH - o) * BR, BR)],
                send_sem=hs_sem.at[rd],
                recv_sem=hr_sem.at[rd],
                device_id=halo_dev(o),
                device_id_type=MESH,
            ).start()

    def wait_bytes(ref, sem):
        pltpu.make_async_copy(ref, ref, sem).wait()

    def halo_wait(rd):
        wait_bytes(win.at[rd, pl.ds(0, WIN - BR)], hr_sem.at[rd])

    def near_send(gm, value):
        lanes = value.shape[1]
        msg[gm, 0] = jnp.concatenate([value, jnp.zeros((COLS, TB - lanes), F32)], axis=1)
        near[gm, pos] = msg[gm, 0]
        for n in range(1, CELL):
            pltpu.make_async_remote_copy(
                src_ref=msg.at[gm, 0],
                dst_ref=near.at[gm, pos],
                send_sem=ns_sem.at[gm],
                recv_sem=nr_sem.at[gm],
                device_id=near_dev(n),
                device_id_type=MESH,
            ).start()

    def far_send(gm):
        wait_bytes(near.at[gm, pl.ds(0, CELL - 1)], nr_sem.at[gm])
        total = near[gm, 0]
        for n in range(1, CELL):
            total = total + near[gm, n]
        msg[gm, 1] = total
        fars[gm][my_far] = total
        for n in range(1, FAR):
            pltpu.make_async_remote_copy(
                src_ref=msg.at[gm, 1],
                dst_ref=fars[gm].at[my_far],
                send_sem=fs_sem.at[gm],
                recv_sem=fr_sem.at[gm],
                device_id=far_dev(n),
                device_id_type=MESH,
            ).start()

    def far_wait(gm):
        wait_bytes(fars[gm].at[pl.ds(0, FAR - 1)], fr_sem.at[gm])

    def far_all(gm):
        far_wait(gm)
        total = fars[gm][0]
        for n in range(1, FAR):
            total = total + fars[gm][n]
        return total

    lost = lax.rem(lost_ref[0], N_GRP)

    def far_lost(gm):
        far_wait(gm)
        total = fars[gm][lost * (N_ROW // CELL)]
        for n in range(1, N_ROW // CELL):
            total = total + fars[gm][lost * (N_ROW // CELL) + n]
        return total

    def prepare(rd):
        for p in range(2 * REACH + 1):
            group = lax.rem(d + (p - REACH) + N_GRP * N_ROW, N_GRP * N_ROW) // N_ROW
            own = jnp.where(group == g, 1.0, 0.0).astype(F32)
            for q in range(BR):
                x = win[rd, p * BR + q]
                hi, lo = split(x)
                hi_own = hi * own.astype(BF16)
                lo_own = lo * own.astype(BF16)
                winb[p * BR + q] = jnp.concatenate([hi_own, lo_own, hi - hi_own, lo - lo_own], axis=0)

    def product(rd):
        halo_wait(rd)
        prepare(rd)
        own, other = [], []
        for i in range(BR):
            for k in range(K):
                rhs[i, :, k * TB : (k + 1) * TB] = winb[local[i, k]]
            o = lax.dot_general(hl[i], rhs[i], (((1,), (1,)), ((), ())), preferred_element_type=F32)
            o = (o[:TB] + o[TB:]).T
            own.append(o[:COLS] + o[COLS : 2 * COLS])
            other.append(o[2 * COLS : 3 * COLS] + o[3 * COLS :])
        return jnp.concatenate(own, axis=1), jnp.concatenate(other, axis=1)

    def condition(v):
        out = []
        for i in range(BR):
            hi, lo = split(v[:, i * TB : (i + 1) * TB])
            o = lax.dot_general(
                zhl[i], jnp.concatenate([hi, lo], axis=0), (((1,), (1,)), ((), ())), preferred_element_type=F32
            )
            o = (o[:TB] + o[TB:]).T
            out.append(o[:COLS] + o[COLS:])
        return jnp.concatenate(out, axis=1)

    def put(rd, v):
        for i in range(BR):
            win[rd, BAND + i] = v[:, i * TB : (i + 1) * TB]

    def lanes(m, *spans):
        return jnp.concatenate([m[a : a + COLS, b : b + n] for a, b, n in spans], axis=1)

    halo_send(0)
    for i in range(BR):
        pltpu.make_async_copy(tiles_ref.at[i], stage.at[i], load_sem.at[i]).wait()

        def convert(k, carry, i=i):
            hi, lo = split(stage[i, k])
            at = pl.ds(pl.multiple_of(k * TB, TB), TB)
            hl[i, 0:TB, at] = hi
            hl[i, TB : 2 * TB, at] = lo
            return carry

        lax.fori_loop(0, K, convert, 0)
    pltpu.make_async_copy(pre_ref, zstage, load_sem.at[BR]).wait()
    for i in range(BR):
        hi, lo = split(zstage[i])
        zhl[i, 0:TB] = hi
        zhl[i, TB : 2 * TB] = lo
    v0 = flat(b_ref)
    own, p0 = product(0)
    v1 = own + p0 - v0
    put(1, v1)
    halo_send(1)
    basis = jnp.concatenate([v0, v1], axis=0)
    ga = mm(basis, basis, 1, 1)
    near_send(0, lanes(ga, (0, 0, 32), (16, 0, 32)))
    far_send(0)
    own, p1 = product(1)
    v2 = own + p1 - v1
    gb = mm(basis, v2, 1, 1)
    near_send(1, lanes(gb, (0, 0, 16), (16, 0, 16)))
    one = eye16()
    ga = far_all(0)
    ga = jnp.concatenate([ga[:, 0:32], ga[:, 32:64]], axis=0)
    g00 = sym(ga[0:16, 0:16])
    half = sym(ga[0:16, 16:32])
    e0, inv0 = eliminate((g00 + half, half), (g00, one))
    a0 = one - e0
    c = jnp.concatenate([e0, -a0], axis=0)
    squares = mm(c, mm(ga, c), 0, 0)
    m0 = mm(inv0, squares)
    far_send(1)
    d0 = e0 + m0
    d1 = -a0
    dd = jnp.concatenate([d0, d1], axis=0)
    curve = mm(dd, mm(ga, jnp.concatenate([d0, d0 + d1], axis=0)), 0, 0)
    gb = far_all(1)
    gb = jnp.concatenate([gb[:, 0:16], gb[:, 16:32]], axis=0)
    curve = curve + mm(dd, mm(gb, d1), 0, 0)
    (a1,) = eliminate((sym(curve), squares))
    cs = mm(dd, a1) + jnp.concatenate([a0, jnp.zeros_like(a0)], axis=0)
    coupled = mm(cs, jnp.concatenate([p0, p1], axis=0), 0, 0)
    rr = v0 - coupled
    s0 = condition(rr)
    put(2, s0)
    halo_send(2)
    base_rec = mm(cs, basis, 0, 0)
    d0a = mm(d0, a1)
    d1a = mm(d1, a1)
    rc = jnp.concatenate([e0 - d0a, -(a0 + d0a + d1a), -d1a], axis=0)
    residual = mm(rc, jnp.concatenate([v0, v1, v2], axis=0), 0, 0)
    q0, ps0 = product(2)
    t0 = condition(q0)
    put(3, t0)
    halo_send(3)
    g2 = mm(jnp.concatenate([rr, s0, q0], axis=0), jnp.concatenate([s0, q0, t0], axis=0), 1, 1)
    near_send(2, lanes(g2, (0, 0, 16), (0, 32, 16), (16, 16, 16), (32, 32, 16)))
    far_send(2)
    q1, ps1 = product(3)
    st = jnp.concatenate([s0, t0], axis=0)
    g3 = mm(st, q1, 1, 1)
    near_send(3, lanes(g3, (0, 0, 16), (16, 0, 16)))
    g2 = far_lost(2)
    w0 = g2[:, 0:16]
    rt, sq, qt = g2[:, 16:32], g2[:, 32:48], g2[:, 48:64]
    b0, invw = eliminate((sym(sq), w0), (sym(w0), one))
    w1 = w0 - mm(rt, b0) + mm(b0, mm(qt, b0) - sq.T, 0, 0)
    n0 = one + mm(invw, w1)
    far_send(3)
    nb = jnp.concatenate([n0, -b0], axis=0)
    bend = mm(nb, mm(jnp.concatenate([sq, qt.T], axis=0), n0), 0, 0)
    side = jnp.where(r < N_ROW // 2, g - 1, g + 1)
    is_lost = g == lost
    touch = jnp.where(side == lost, 1.0, 0.0).astype(F32)
    base = jnp.where(is_lost, rr, residual + touch * coupled)
    xa = jnp.where(is_lost, q0, touch * ps0)
    xb = jnp.where(is_lost, q1, touch * ps1)
    xs = jnp.concatenate([xa, xb], axis=0)
    g3 = far_lost(3)
    g3 = jnp.concatenate([g3[:, 0:16], g3[:, 16:32]], axis=0)
    bend = bend - mm(nb, mm(g3, b0), 0, 0)
    (b1,) = eliminate((sym(bend), w1))
    es = mm(nb, b1) + jnp.concatenate([b0, jnp.zeros_like(b0)], axis=0)
    rec = jnp.where(is_lost, mm(es, st, 0, 0), base_rec)
    tres = base - mm(es, xs, 0, 0)
    for i in range(BR):
        rec_ref[i] = rec[:, i * TB : (i + 1) * TB]
        tres_ref[i] = tres[:, i * TB : (i + 1) * TB]
    for rd in range(4):
        wait_bytes(win.at[rd, pl.ds(0, WIN - BR)], hs_sem.at[rd])
        wait_bytes(near.at[rd, pl.ds(0, CELL - 1)], ns_sem.at[rd])
        wait_bytes(fars[rd].at[pl.ds(0, FAR - 1)], fs_sem.at[rd])


def per_device(matrix_tiles, column_index, precond, right_side, lost_group):
    vmem = pl.BlockSpec(memory_space=pltpu.VMEM)
    smem = pl.BlockSpec(memory_space=pltpu.SMEM)
    hbm = pl.BlockSpec(memory_space=pl.ANY)
    shape = jax.ShapeDtypeStruct((BR, COLS, TB), F32)
    dma = pltpu.SemaphoreType.DMA
    return pl.pallas_call(
        kernel,
        out_shape=(shape, shape),
        in_specs=[smem, smem, hbm, hbm, vmem],
        out_specs=(vmem, vmem),
        scratch_shapes=[
            pltpu.VMEM((BR, K, TB, TB), F32),
            pltpu.VMEM((BR, TB, TB), F32),
            pltpu.VMEM((BR, 2 * TB, K * TB), BF16),
            pltpu.VMEM((BR, 2 * TB, TB), BF16),
            pltpu.VMEM((4, WIN, COLS, TB), F32),
            pltpu.VMEM((WIN, 4 * COLS, TB), BF16),
            pltpu.VMEM((BR, 4 * COLS, K * TB), BF16),
            pltpu.VMEM((4, 2, COLS, TB), F32),
            pltpu.VMEM((4, CELL, COLS, TB), F32),
            pltpu.VMEM((FAR, COLS, TB), F32),
            pltpu.VMEM((FAR, COLS, TB), F32),
            pltpu.VMEM((FAR, COLS, TB), F32),
            pltpu.VMEM((FAR, COLS, TB), F32),
            pltpu.SMEM((BR, K), jnp.int32),
            dma((BR + 1,)),
            dma((4,)),
            dma((4,)),
            dma((4,)),
            dma((4,)),
            dma((4,)),
            dma((4,)),
        ],
        compiler_params=pltpu.CompilerParams(
            collective_id=0, has_side_effects=True, vmem_limit_bytes=48 * 2**20
        ),
        name="recover",
    )(column_index, lost_group, matrix_tiles, precond, right_side)


def solution(mesh):
    in_specs = (
        P(("grp", "row"), None, None, None),
        P(("grp", "row"), None),
        P(("grp", "row"), None, None),
        P(("grp", "row"), None, None),
        P(),
    )
    out_specs = (P(("grp", "row"), None, None), P(("grp", "row"), None, None))
    return jax.shard_map(
        per_device, mesh=mesh, in_specs=in_specs, out_specs=out_specs, check_vma=False
    )
```

time: 687 us -> 71.1 us (0.10); the launches traced: 676 us -> 70.8 us
  blocking collectives: 472 us -> 0 us
  starting transfers between devices: 101 us -> 0 us
  Pallas kernels: 0 us -> 65.9 us
  matrix products: 63.8 us -> 0 us
  other arithmetic: 24.9 us -> 0 us
    psum x6 -> x0, blocking collectives: 472 us -> none  [the longest x1 125 us: per_device(): weight = lax.psum(inner_products(remainder, smoothed), 'row')]
    ppermute x36 -> x0, starting transfers between devices: 101 us -> none  [from_behind(): lax.ppermute(value, axis, [(source, source + steps) for source in range(f...]
    pallas_call x0 -> x1, Pallas kernels: none -> 65.9 us  [per_device(): pl.pallas_call(kernel, out_shape=(shape, shape), in_specs=[smem, smem, hb...]
    dot_general x24 -> x0, matrix products: 61.3 us -> none  [the longest x6 57 us: tile_product(): jnp.einsum('ikab,ikcb->ica', matrix_tiles, picked, precision=lax.Precisio...]
    another operation x30 -> x0, other arithmetic: 24.1 us -> none  [the longest x18 12.8 us: solve_sym(): factor = jnp.linalg.cholesky(0.5 * (matrix + matrix.T))]
  transfers between devices with their start and end apart: 36 -> 0, of which waited for: 6 -> 0; matrix products, arithmetic and copies ran while one was open for 0% -> 0% of each run, Pallas kernels for 0% -> 0%
where the time goes in v1:
time: 71.1 us; the launch traced here: 70.8 us
  Pallas kernels  65.9 us (93%)
  local copies, waits for them, and re-layouts  3.61 us (5%)
  between operations  1.3 us (2%)
    pallas_call x1, Pallas kernels, per_device(): pl.pallas_call(kernel, out_shape=(shape, shape), in_specs=[smem, smem, hb...  65.9 us
    unnamed x8, local copies, waits for them, and re-layouts  3.61 us

profile of v1, /device:TPU:1, one launch (start us, length us, event | category | flops | bytes accessed | tf_op | source)
XLA Modules:
  0.0 70.8 jit_solution(13611793964855196700)
XLA Ops:
  1.3 0.0 copy-start
  1.3 0.9 %copy-done = f32[4,128,128]{2,1,0:T(8,128)S(1)} copy-done((f32[4,128,128]{2,1,0:T(8,128)S(1)}, f32[4,128,128]{2,1,0:T(8,128)}, u32[]{:S(2)}) %copy-start) | copy-done | bytes 262168
  2.2 0.0 copy-start.1
  2.2 0.8 %copy-done.1 = f32[4,16,128]{2,1,0:T(8,128)S(1)} copy-done((f32[4,16,128]{2,1,0:T(8,128)S(1)}, f32[4,16,128]{2,1,0:T(8,128)}, u32[]{:S(2)}) %copy-start.1) | copy-done | bytes 32792
  3.0 0.0 copy-start.2
  3.0 0.7 copy-done.2
  3.7 65.9 %recover.1 = (f32[4,16,128]{2,1,0:T(8,128)S(1)}, f32[4,16,128]{2,1,0:T(8,128)S(1)}) custom-call(s32[4,32]{1,0:T(4,128)S(1)} %copy-done.2, s32[1]{0:T(128)S(6)} %copy.9.lost_ref, f32[4,32,128,128]{3,2,1,0:T(8,128)} %tiles_ref.1, f32[4,128,128]{2,1,0:T(8,128)S(1)} %copy-done, f32[4,16,128]{2,1,0:T(8,128)S(1)} %copy-done.1), custom_call_target="tpu_custom_call" | custom-call | tf_op jit(solution)/shard_map/recover/pallas_call | solution.py:322
  69.6 0.6 copy.10
  70.2 0.6 copy.11
Async XLA Ops:
  1.3 1.0 %copy-start = (f32[4,128,128]{2,1,0:T(8,128)S(1)}, f32[4,128,128]{2,1,0:T(8,128)}, u32[]{:S(2)}) copy-start(f32[4,128,128]{2,1,0:T(8,128)} %pre_ref.1) | copy-start | bytes 786436
  2.2 0.8 %copy-start.1 = (f32[4,16,128]{2,1,0:T(8,128)S(1)}, f32[4,16,128]{2,1,0:T(8,128)}, u32[]{:S(2)}) copy-start(f32[4,16,128]{2,1,0:T(8,128)} %b_ref.1) | copy-start | bytes 98308
  3.0 0.7 copy-start.2

commit v2 on v1

v2 whole, which is shorter than its diff:
```python
import functools

import jax
import jax.numpy as jnp
from jax import lax
from jax.experimental import pallas as pl
from jax.experimental.pallas import tpu as pltpu
from jax.sharding import PartitionSpec as P

BAND = 12
F32 = jnp.float32
BF16 = jnp.bfloat16
MESH = pl.DeviceIdType.MESH
N_GRP, N_ROW, BR, K, COLS, TB = 4, 32, 4, 32, 16, 128
REACH = 3
WIN = BR * (2 * REACH + 1)
CELL = 8
FAR = (N_GRP * N_ROW) // CELL
CELLS = N_ROW // CELL
WB, WZ, WV, WP, WQ, WT = range(6)
WINS = 6


def mm(a, b, ca=1, cb=0):
    return lax.dot_general(
        a, b, (((ca,), (cb,)), ((), ())), precision=lax.Precision.HIGHEST, preferred_element_type=F32
    )


def split(x):
    hi = x.astype(BF16)
    return hi, (x - hi.astype(F32)).astype(BF16)


def eye16():
    r = lax.broadcasted_iota(jnp.int32, (COLS, COLS), 0)
    c = lax.broadcasted_iota(jnp.int32, (COLS, COLS), 1)
    return (r == c).astype(F32)


def sym(g):
    return 0.5 * (g + g.T)


def eliminate(*systems):
    mats = [jnp.concatenate([s, h], axis=1) for s, h in systems]
    rows = lax.broadcasted_iota(jnp.int32, mats[0].shape, 0)
    for j in range(COLS):
        for n, m in enumerate(mats):
            row = m[j : j + 1, :] / m[j : j + 1, j : j + 1]
            mats[n] = jnp.where(rows == j, row, m - m[:, j : j + 1] * row)
    return [m[:, COLS:] for m in mats]


def flat(v):
    return jnp.concatenate([v[i] for i in range(BR)], axis=1)


def kernel(
    cols_hbm, lost_hbm, tiles_ref, pre_hbm, b_hbm, rec_ref, tres_ref,
    stage, zstage, hl, zhl, win, winb, winc, rhs, msg, near, far0, far1, side2, side3, cols_ref, lost_ref, local,
    load_sem, hs_sem, hr_sem, ns_sem, nr_sem, fs_sem, fr_sem, as_sem, ar_sem,
):
    g = lax.axis_index("grp")
    r = lax.axis_index("row")
    d = g * N_ROW + r
    cell = r // CELL
    pos = lax.rem(r, CELL)
    my_far = g * CELLS + cell
    first = d * BR - BAND
    total_devices = N_GRP * N_ROW

    def near_dev(n):
        return (g, cell * CELL + lax.rem(pos + n, CELL))

    def far_dev(n):
        f = lax.rem(my_far + n, FAR)
        return (f // CELLS, lax.rem(f, CELLS) * CELL + pos)

    def halo_dev(o):
        t = lax.rem(d + o + total_devices, total_devices)
        return (t // N_ROW, lax.rem(t, N_ROW))

    offsets = [3, -3, 2, -2, 1, -1]
    fars = [far0, far1]
    sides = [side2, side3]

    for side in sides:
        for n in range(CELLS):
            side[CELLS + n] = jnp.zeros((COLS, TB), F32)

    barrier = pltpu.get_barrier_semaphore()
    for o in offsets:
        pl.semaphore_signal(barrier, inc=1, device_id=halo_dev(o), device_id_type=MESH)
    for n in range(1, FAR):
        pl.semaphore_signal(barrier, inc=1, device_id=far_dev(n), device_id_type=MESH)
    for n in range(1, CELL):
        pl.semaphore_signal(barrier, inc=1, device_id=near_dev(n), device_id_type=MESH)

    own_span = pl.ds(BAND, BR)
    loads = [
        pltpu.make_async_copy(b_hbm, win.at[WB, own_span], load_sem.at[0]),
        pltpu.make_async_copy(pre_hbm, zstage, load_sem.at[1]),
        pltpu.make_async_copy(cols_hbm, cols_ref, load_sem.at[2]),
        pltpu.make_async_copy(lost_hbm, lost_ref, load_sem.at[3]),
    ] + [pltpu.make_async_copy(tiles_ref.at[i], stage.at[i], load_sem.at[4 + i]) for i in range(BR)]
    for load in loads:
        load.start()

    def wait_bytes(ref, sem):
        pltpu.make_async_copy(ref, ref, sem).wait()

    def halo_send(w):
        for o in offsets:
            pltpu.make_async_remote_copy(
                src_ref=win.at[w, own_span],
                dst_ref=win.at[w, pl.ds((REACH - o) * BR, BR)],
                send_sem=hs_sem.at[w],
                recv_sem=hr_sem.at[w],
                device_id=halo_dev(o),
                device_id_type=MESH,
            ).start()

    def halo_wait(w):
        wait_bytes(win.at[w, pl.ds(0, WIN - BR)], hr_sem.at[w])

    def near_send(gm, value):
        n_lanes = value.shape[1]
        value = jnp.concatenate([value, jnp.zeros((COLS, TB - n_lanes), F32)], axis=1)
        msg[gm, 0] = value
        near[gm, pos] = value
        for n in range(1, CELL):
            pltpu.make_async_remote_copy(
                src_ref=msg.at[gm, 0],
                dst_ref=near.at[gm, pos],
                send_sem=ns_sem.at[gm],
                recv_sem=nr_sem.at[gm],
                device_id=near_dev(n),
                device_id_type=MESH,
            ).start()

    def near_sum(gm):
        wait_bytes(near.at[gm, pl.ds(0, CELL - 1)], nr_sem.at[gm])
        terms = [near[gm, n] for n in range(CELL)]
        while len(terms) > 1:
            terms = [terms[n] + terms[n + 1] for n in range(0, len(terms), 2)]
        msg[gm, 1] = terms[0]
        return terms[0]

    def far_send(gm):
        far = fars[gm]
        far[my_far] = near_sum(gm)
        for n in range(1, FAR):
            pltpu.make_async_remote_copy(
                src_ref=msg.at[gm, 1],
                dst_ref=far.at[my_far],
                send_sem=fs_sem.at[gm],
                recv_sem=fr_sem.at[gm],
                device_id=far_dev(n),
                device_id_type=MESH,
            ).start()

    def far_all(gm):
        far = fars[gm]
        wait_bytes(far.at[pl.ds(0, FAR - 1)], fr_sem.at[gm])
        terms = [far[n] for n in range(FAR)]
        while len(terms) > 1:
            terms = [terms[n] + terms[n + 1] for n in range(0, len(terms), 2)]
        return terms[0]

    def side_send(gm):
        side = sides[gm - 2]
        side[cell] = near_sum(gm)
        for n in range(1, CELLS):
            pltpu.make_async_remote_copy(
                src_ref=msg.at[gm, 1],
                dst_ref=side.at[cell],
                send_sem=fs_sem.at[gm],
                recv_sem=fr_sem.at[gm],
                device_id=(g, lax.rem(cell + n, CELLS) * CELL + pos),
                device_id_type=MESH,
            ).start()
        for step, target in ((1, 0), (N_GRP - 1, CELLS - 1)):
            pltpu.make_async_remote_copy(
                src_ref=msg.at[gm, 1],
                dst_ref=side.at[CELLS + cell],
                send_sem=as_sem.at[gm - 2],
                recv_sem=ar_sem.at[gm - 2],
                device_id=(lax.rem(g + step, N_GRP), target * CELL + pos),
                device_id_type=MESH,
            ).start()

    lost_of = [None]

    def side_sum(gm):
        side = sides[gm - 2]
        wait_bytes(side.at[pl.ds(0, CELLS - 1)], fr_sem.at[gm])

        @pl.when(jnp.logical_or(cell == 0, cell == CELLS - 1))
        def _():
            wait_bytes(side.at[pl.ds(0, CELLS)], ar_sem.at[gm - 2])

        own = (side[0] + side[1]) + (side[2] + side[3])
        other = (side[4] + side[5]) + (side[6] + side[7])
        return jnp.where(lost_of[0], other, own)

    def prepare(w, ref, at):
        for p in range(2 * REACH + 1):
            group = lax.rem(d + (p - REACH) + total_devices, total_devices) // N_ROW
            own = jnp.where(group == g, 1.0, 0.0).astype(BF16)
            for q in range(BR):
                hi, lo = split(win[w, p * BR + q])
                hi_own = hi * own
                lo_own = lo * own
                ref[p * BR + q, at : at + 4 * COLS] = jnp.concatenate(
                    [hi_own, lo_own, hi - hi_own, lo - lo_own], axis=0
                )

    def product(ref, count):
        own = [[] for _ in range(count)]
        other = [[] for _ in range(count)]
        rows = 4 * COLS * count
        for i in range(BR):
            for k in range(K):
                rhs[i, 0:rows, k * TB : (k + 1) * TB] = ref[local[i, k]]
            o = lax.dot_general(hl[i], rhs[i, 0:rows], (((1,), (1,)), ((), ())), preferred_element_type=F32)
            o = (o[:TB] + o[TB:]).T
            for n in range(count):
                own[n].append(o[4 * n * COLS : (4 * n + 1) * COLS] + o[(4 * n + 1) * COLS : (4 * n + 2) * COLS])
                other[n].append(
                    o[(4 * n + 2) * COLS : (4 * n + 3) * COLS] + o[(4 * n + 3) * COLS : (4 * n + 4) * COLS]
                )
        return [jnp.concatenate(v, axis=1) for v in own], [jnp.concatenate(v, axis=1) for v in other]

    def condition(*vectors):
        out = [[] for _ in vectors]
        for i in range(BR):
            parts = []
            for v in vectors:
                parts.extend(split(v[:, i * TB : (i + 1) * TB]))
            o = lax.dot_general(
                zhl[i], jnp.concatenate(parts, axis=0), (((1,), (1,)), ((), ())), preferred_element_type=F32
            )
            o = (o[:TB] + o[TB:]).T
            for n in range(len(vectors)):
                out[n].append(o[2 * n * COLS : (2 * n + 1) * COLS] + o[(2 * n + 1) * COLS : (2 * n + 2) * COLS])
        return [jnp.concatenate(v, axis=1) for v in out]

    def put(w, v):
        for i in range(BR):
            win[w, BAND + i] = v[:, i * TB : (i + 1) * TB]

    def lanes(m, *spans):
        return jnp.concatenate([m[a : a + COLS, b : b + n] for a, b, n in spans], axis=1)

    def stack(*parts):
        return jnp.concatenate(parts, axis=0)

    loads[0].wait()
    pl.semaphore_wait(barrier, len(offsets) + CELL - 1 + FAR - 1)
    halo_send(WB)
    loads[1].wait()
    for i in range(BR):
        hi, lo = split(zstage[i])
        zhl[i, 0:TB] = hi
        zhl[i, TB : 2 * TB] = lo
    v0 = jnp.concatenate([win[WB, BAND + i] for i in range(BR)], axis=1)
    (zb,) = condition(v0)
    put(WZ, zb)
    halo_send(WZ)
    loads[2].wait()

    def localise(k, carry):
        for i in range(BR):
            local[i, k] = jnp.clip(cols_ref[i, k] - first, 0, WIN - 1)
        return carry

    lax.fori_loop(0, K, localise, 0)
    for i in range(BR):
        loads[4 + i].wait()

        def convert(k, carry, i=i):
            hi, lo = split(stage[i, k])
            at = pl.ds(pl.multiple_of(k * TB, TB), TB)
            hl[i, 0:TB, at] = hi
            hl[i, TB : 2 * TB, at] = lo
            return carry

        lax.fori_loop(0, K, convert, 0)
    halo_wait(WB)
    prepare(WB, winb, 0)
    (own,), (p0,) = product(winb, 1)
    v1 = own + p0 - v0
    put(WV, v1)
    halo_send(WV)
    (zp0,) = condition(p0)
    put(WP, zp0)
    halo_send(WP)
    basis = stack(v0, v1)
    ga = mm(basis, basis, 1, 1)
    near_send(0, lanes(ga, (0, 0, 32), (16, 0, 32)))
    loads[3].wait()
    lost = lax.rem(lost_ref[0], N_GRP)
    edge = jnp.logical_or(cell == 0, cell == CELLS - 1)
    touch = jnp.logical_and(edge, jnp.where(r < N_ROW // 2, g - 1, g + 1) == lost)
    is_lost = g == lost
    lost_of[0] = touch
    halo_wait(WZ)
    prepare(WZ, winc, 0)
    far_send(0)
    halo_wait(WV)
    prepare(WV, winb, 0)
    (own,), (p1,) = product(winb, 1)
    (zp1,) = condition(p1)
    put(WQ, zp1)
    halo_send(WQ)
    v2 = own + p1 - v1
    gb = mm(basis, v2, 1, 1)
    near_send(1, lanes(gb, (0, 0, 16), (16, 0, 16)))
    one = eye16()
    ga = far_all(0)
    ga = stack(ga[:, 0:32], ga[:, 32:64])
    g00 = sym(ga[0:16, 0:16])
    half = sym(ga[0:16, 16:32])
    e0, inv0 = eliminate((g00 + half, half), (g00, one))
    a0 = one - e0
    c = stack(e0, -a0)
    squares = mm(c, mm(ga, c), 0, 0)
    far_send(1)
    m0 = mm(inv0, squares)
    d0 = e0 + m0
    d1 = -a0
    dd = stack(d0, d1)
    curve = mm(dd, mm(ga, stack(d0, d0 + d1)), 0, 0)
    halo_wait(WP)
    prepare(WP, winc, 4 * COLS)
    halo_wait(WQ)
    prepare(WQ, winc, 8 * COLS)
    (bz, bzp0, bzp1), (oz, ozp0, ozp1) = product(winc, 3)
    y, yp0, yp1 = condition(bz, bzp0, bzp1)
    gb = far_all(1)
    gb = stack(gb[:, 0:16], gb[:, 16:32])
    curve = curve + mm(dd, mm(gb, d1), 0, 0)
    (a1,) = eliminate((sym(curve), squares))
    cs = mm(dd, a1) + stack(a0, jnp.zeros_like(a0))
    t0 = y - mm(cs, stack(yp0, yp1), 0, 0)
    put(WT, t0)
    halo_send(WT)
    coupled = mm(cs, stack(p0, p1), 0, 0)
    rr = v0 - coupled
    s0 = zb - mm(cs, stack(zp0, zp1), 0, 0)
    q0 = bz - mm(cs, stack(bzp0, bzp1), 0, 0)
    g2 = mm(stack(rr, s0, q0), stack(s0, q0, t0), 1, 1)
    near_send(2, lanes(g2, (0, 0, 16), (0, 32, 16), (16, 16, 16), (32, 32, 16)))
    ps0 = oz - mm(cs, stack(ozp0, ozp1), 0, 0)
    base_rec = mm(cs, basis, 0, 0)
    d0a = mm(d0, a1)
    d1a = mm(d1, a1)
    rc = stack(e0 - d0a, -(a0 + d0a + d1a), -d1a)
    residual = mm(rc, stack(v0, v1, v2), 0, 0)
    st = stack(s0, t0)
    side_send(2)
    halo_wait(WT)
    prepare(WT, winb, 0)
    (q1,), (ps1,) = product(winb, 1)
    g3 = mm(st, q1, 1, 1)
    near_send(3, lanes(g3, (0, 0, 16), (16, 0, 16)))
    g2 = side_sum(2)
    w0 = g2[:, 0:16]
    rt, sq, qt = g2[:, 16:32], g2[:, 32:48], g2[:, 48:64]
    b0, invw = eliminate((sym(sq), w0), (sym(w0), one))
    w1 = w0 - mm(rt, b0) + mm(b0, mm(qt, b0) - sq.T, 0, 0)
    side_send(3)
    n0 = one + mm(invw, w1)
    nb = stack(n0, -b0)
    bend = mm(nb, mm(stack(sq, qt.T), n0), 0, 0)
    base = jnp.where(is_lost, rr, residual + jnp.where(touch, coupled, 0.0))
    xs = stack(jnp.where(is_lost, q0, ps0), jnp.where(is_lost, q1, ps1))
    g3 = side_sum(3)
    g3 = stack(g3[:, 0:16], g3[:, 16:32])
    bend = bend - mm(nb, mm(g3, b0), 0, 0)
    (b1,) = eliminate((sym(bend), w1))
    es = mm(nb, b1) + stack(b0, jnp.zeros_like(b0))
    rec = jnp.where(is_lost, mm(es, st, 0, 0), base_rec)
    tres = jnp.where(jnp.logical_or(is_lost, touch), base - mm(es, xs, 0, 0), base)
    for i in range(BR):
        rec_ref[i] = rec[:, i * TB : (i + 1) * TB]
        tres_ref[i] = tres[:, i * TB : (i + 1) * TB]
    for w in range(WINS):
        wait_bytes(win.at[w, pl.ds(0, WIN - BR)], hs_sem.at[w])
    for gm in range(4):
        wait_bytes(near.at[gm, pl.ds(0, CELL - 1)], ns_sem.at[gm])
    for gm in range(2):
        wait_bytes(fars[gm].at[pl.ds(0, FAR - 1)], fs_sem.at[gm])
        wait_bytes(sides[gm].at[pl.ds(0, CELLS - 1)], fs_sem.at[gm + 2])
        wait_bytes(sides[gm].at[pl.ds(0, 2)], as_sem.at[gm])


def per_device(matrix_tiles, column_index, precond, right_side, lost_group):
    vmem = pl.BlockSpec(memory_space=pltpu.VMEM)
    hbm = pl.BlockSpec(memory_space=pltpu.HBM)
    shape = jax.ShapeDtypeStruct((BR, COLS, TB), F32)
    dma = pltpu.SemaphoreType.DMA
    return pl.pallas_call(
        kernel,
        out_shape=(shape, shape),
        in_specs=[hbm, hbm, hbm, hbm, hbm],
        out_specs=(vmem, vmem),
        scratch_shapes=[
            pltpu.VMEM((BR, K, TB, TB), F32),
            pltpu.VMEM((BR, TB, TB), F32),
            pltpu.VMEM((BR, 2 * TB, K * TB), BF16),
            pltpu.VMEM((BR, 2 * TB, TB), BF16),
            pltpu.VMEM((WINS, WIN, COLS, TB), F32),
            pltpu.VMEM((WIN, 4 * COLS, TB), BF16),
            pltpu.VMEM((WIN, 12 * COLS, TB), BF16),
            pltpu.VMEM((BR, 12 * COLS, K * TB), BF16),
            pltpu.VMEM((4, 2, COLS, TB), F32),
            pltpu.VMEM((4, CELL, COLS, TB), F32),
            pltpu.VMEM((FAR, COLS, TB), F32),
            pltpu.VMEM((FAR, COLS, TB), F32),
            pltpu.VMEM((2 * CELLS, COLS, TB), F32),
            pltpu.VMEM((2 * CELLS, COLS, TB), F32),
            pltpu.SMEM((BR, K), jnp.int32),
            pltpu.SMEM((1,), jnp.int32),
            pltpu.SMEM((BR, K), jnp.int32),
            dma((4 + BR,)),
            dma((WINS,)),
            dma((WINS,)),
            dma((4,)),
            dma((4,)),
            dma((4,)),
            dma((4,)),
            dma((2,)),
            dma((2,)),
        ],
        compiler_params=pltpu.CompilerParams(
            collective_id=0, has_side_effects=True, vmem_limit_bytes=int(64 * 2**20)
        ),
        name="recover",
    )(column_index, lost_group, matrix_tiles, precond, right_side)


def solution(mesh):
    in_specs = (
        P(("grp", "row"), None, None, None),
        P(("grp", "row"), None),
        P(("grp", "row"), None, None),
        P(("grp", "row"), None, None),
        P(),
    )
    out_specs = (P(("grp", "row"), None, None), P(("grp", "row"), None, None))
    return jax.shard_map(
        per_device, mesh=mesh, in_specs=in_specs, out_specs=out_specs, check_vma=False
    )
```

time: 71.1 us -> 64.9 us (0.913)
  Pallas kernels: 65.9 us -> 60.6 us
  local copies, waits for them, and re-layouts: 3.61 us -> 2.75 us
    pallas_call x1, Pallas kernels: 65.9 us -> 60.6 us  [per_device(): pl.pallas_call(kernel, out_shape=(shape, shape), in_specs=[hbm, hbm, hbm,...]
    unnamed x8 -> x2, local copies, waits for them, and re-layouts: 3.61 us -> 2.75 us
where the time goes in v2:
time: 64.9 us; the launch traced here: 64.6 us
  Pallas kernels  60.6 us (93%)
  local copies, waits for them, and re-layouts  2.75 us (4%)
  between operations  1.29 us (2%)
    pallas_call x1, Pallas kernels, per_device(): pl.pallas_call(kernel, out_shape=(shape, shape), in_specs=[hbm, hbm, hbm,...  60.6 us
    unnamed x2, local copies, waits for them, and re-layouts  2.75 us

profile of v2, /device:TPU:1, one launch (start us, length us, event | category | flops | bytes accessed | tf_op | source)
XLA Modules:
  0.0 64.6 jit_solution(4589484479145678008)
XLA Ops:
  1.3 60.6 %recover.1 = (f32[4,16,128]{2,1,0:T(8,128)}, f32[4,16,128]{2,1,0:T(8,128)}) custom-call(s32[4,32]{1,0:T(4,128)} %cols_hbm.1, s32[1]{0:T(128)S(6)} %copy.9.lost_hbm, f32[4,32,128,128]{3,2,1,0:T(8,128)} %tiles_ref.1, f32[4,128,128]{2,1,0:T(8,128)} %pre_hbm.1, f32[4,16,128]{2,1,0:T(8,128)} %b_hbm.1), custom_call_target="tpu_custom_call" | custom-call | tf_op jit(solution)/shard_map/recover/pallas_call | solution.py:404
  61.9 1.4 %copy.10 = f32[4,16,128]{2,1,0:T(8,128)} copy(f32[4,16,128]{2,1,0:T(8,128)} %get-tuple-element.4) | data formatting | bytes 65536
  63.3 1.4 %copy.11 = f32[4,16,128]{2,1,0:T(8,128)} copy(f32[4,16,128]{2,1,0:T(8,128)} %get-tuple-element.5) | data formatting | bytes 65536

commit v3 on v2

--- a/solution.py
+++ b/solution.py
@@ -44,21 +44,27 @@
 
 def eliminate(*systems):
     mats = [jnp.concatenate([s, h], axis=1) for s, h in systems]
-    rows = lax.broadcasted_iota(jnp.int32, mats[0].shape, 0)
+    shape = mats[0].shape
+    rows = lax.broadcasted_iota(jnp.int32, shape, 0)
+    columns = [[jnp.broadcast_to(m[:, j : j + 1], shape) for j in range(COLS)] for m in mats]
+
+    def step(value, column, inverse, j):
+        row = value[j : j + 1] * inverse
+        return jnp.where(rows == j, row, value - column * row)
+
     for j in range(COLS):
-        for n, m in enumerate(mats):
-            row = m[j : j + 1, :] / m[j : j + 1, j : j + 1]
-            mats[n] = jnp.where(rows == j, row, m - m[:, j : j + 1] * row)
+        for n in range(len(mats)):
+            column = columns[n][j]
+            inverse = 1.0 / column[j : j + 1]
+            mats[n] = step(mats[n], column, inverse, j)
+            for u in range(j + 1, COLS):
+                columns[n][u] = step(columns[n][u], column, inverse, j)
     return [m[:, COLS:] for m in mats]
-
-
-def flat(v):
-    return jnp.concatenate([v[i] for i in range(BR)], axis=1)
 
 
 def kernel(
     cols_hbm, lost_hbm, tiles_ref, pre_hbm, b_hbm, rec_ref, tres_ref,
-    stage, zstage, hl, zhl, win, winb, winc, rhs, msg, near, far0, far1, side2, side3, cols_ref, lost_ref, local,
+    stage, zstage, hl, zhl, win, winb, winc, rhs, msg, near, far0, far1, side, shot, shot_msg, cols_ref, lost_ref, local,
     load_sem, hs_sem, hr_sem, ns_sem, nr_sem, fs_sem, fr_sem, as_sem, ar_sem,
 ):
     g = lax.axis_index("grp")
@@ -81,13 +87,14 @@
         t = lax.rem(d + o + total_devices, total_devices)
         return (t // N_ROW, lax.rem(t, N_ROW))
 
+    border = jnp.logical_or(r < REACH, r >= N_ROW - REACH)
     offsets = [3, -3, 2, -2, 1, -1]
     fars = [far0, far1]
-    sides = [side2, side3]
-
-    for side in sides:
-        for n in range(CELLS):
-            side[CELLS + n] = jnp.zeros((COLS, TB), F32)
+
+    for n in range(CELLS):
+        side[CELLS + n] = jnp.zeros((COLS, TB), F32)
+    for n in range(N_ROW):
+        shot[N_ROW + n] = jnp.zeros((COLS // 2, TB), F32)
 
     barrier = pltpu.get_barrier_semaphore()
     for o in offsets:
@@ -169,7 +176,6 @@
         return terms[0]
 
     def side_send(gm):
-        side = sides[gm - 2]
         side[cell] = near_sum(gm)
         for n in range(1, CELLS):
             pltpu.make_async_remote_copy(
@@ -184,8 +190,8 @@
             pltpu.make_async_remote_copy(
                 src_ref=msg.at[gm, 1],
                 dst_ref=side.at[CELLS + cell],
-                send_sem=as_sem.at[gm - 2],
-                recv_sem=ar_sem.at[gm - 2],
+                send_sem=as_sem.at[0],
+                recv_sem=ar_sem.at[0],
                 device_id=(lax.rem(g + step, N_GRP), target * CELL + pos),
                 device_id_type=MESH,
             ).start()
@@ -193,16 +199,58 @@
     lost_of = [None]
 
     def side_sum(gm):
-        side = sides[gm - 2]
         wait_bytes(side.at[pl.ds(0, CELLS - 1)], fr_sem.at[gm])
 
         @pl.when(jnp.logical_or(cell == 0, cell == CELLS - 1))
         def _():
-            wait_bytes(side.at[pl.ds(0, CELLS)], ar_sem.at[gm - 2])
+            wait_bytes(side.at[pl.ds(0, CELLS)], ar_sem.at[0])
 
         own = (side[0] + side[1]) + (side[2] + side[3])
         other = (side[4] + side[5]) + (side[6] + side[7])
         return jnp.where(lost_of[0], other, own)
+
+    far_edges = [(1, 0), (1, 1), (1, 2), (N_GRP - 1, N_ROW - 1), (N_GRP - 1, N_ROW - 2), (N_GRP - 1, N_ROW - 3)]
+
+    def shot_send(value):
+        half = COLS // 2
+        parts = [value[n * half : (n + 1) * half] for n in range(4)] + [jnp.zeros((half, TB - 4 * COLS), F32)]
+        value = jnp.concatenate(parts, axis=1)
+        shot_msg[...] = value
+        shot[r] = value
+        for n in range(1, N_ROW):
+            pltpu.make_async_remote_copy(
+                src_ref=shot_msg,
+                dst_ref=shot.at[r],
+                send_sem=fs_sem.at[3],
+                recv_sem=fr_sem.at[3],
+                device_id=(g, lax.rem(r + n, N_ROW)),
+                device_id_type=MESH,
+            ).start()
+        for step, target in far_edges:
+            pltpu.make_async_remote_copy(
+                src_ref=shot_msg,
+                dst_ref=shot.at[N_ROW + r],
+                send_sem=as_sem.at[1],
+                recv_sem=ar_sem.at[1],
+                device_id=(lax.rem(g + step, N_GRP), target),
+                device_id_type=MESH,
+            ).start()
+
+    def shot_sum():
+        wait_bytes(shot.at[pl.ds(0, N_ROW - 1)], fr_sem.at[3])
+
+        @pl.when(border)
+        def _():
+            wait_bytes(shot.at[pl.ds(0, N_ROW)], ar_sem.at[1])
+
+        sums = []
+        for at in (0, N_ROW):
+            terms = [shot[at + n] for n in range(N_ROW)]
+            while len(terms) > 1:
+                terms = [terms[n] + terms[n + 1] for n in range(0, len(terms), 2)]
+            sums.append(terms[0])
+        total = jnp.where(lost_of[0], sums[1], sums[0])
+        return jnp.concatenate([total[:, n * COLS : (n + 1) * COLS] for n in range(4)], axis=0)
 
     def prepare(w, ref, at):
         for p in range(2 * REACH + 1):
@@ -301,8 +349,7 @@
     near_send(0, lanes(ga, (0, 0, 32), (16, 0, 32)))
     loads[3].wait()
     lost = lax.rem(lost_ref[0], N_GRP)
-    edge = jnp.logical_or(cell == 0, cell == CELLS - 1)
-    touch = jnp.logical_and(edge, jnp.where(r < N_ROW // 2, g - 1, g + 1) == lost)
+    touch = jnp.logical_and(border, jnp.where(r < N_ROW // 2, g - 1, g + 1) == lost)
     is_lost = g == lost
     lost_of[0] = touch
     halo_wait(WZ)
@@ -364,20 +411,18 @@
     prepare(WT, winb, 0)
     (q1,), (ps1,) = product(winb, 1)
     g3 = mm(st, q1, 1, 1)
-    near_send(3, lanes(g3, (0, 0, 16), (16, 0, 16)))
+    shot_send(g3)
     g2 = side_sum(2)
     w0 = g2[:, 0:16]
     rt, sq, qt = g2[:, 16:32], g2[:, 32:48], g2[:, 48:64]
     b0, invw = eliminate((sym(sq), w0), (sym(w0), one))
     w1 = w0 - mm(rt, b0) + mm(b0, mm(qt, b0) - sq.T, 0, 0)
-    side_send(3)
     n0 = one + mm(invw, w1)
     nb = stack(n0, -b0)
     bend = mm(nb, mm(stack(sq, qt.T), n0), 0, 0)
     base = jnp.where(is_lost, rr, residual + jnp.where(touch, coupled, 0.0))
     xs = stack(jnp.where(is_lost, q0, ps0), jnp.where(is_lost, q1, ps1))
-    g3 = side_sum(3)
-    g3 = stack(g3[:, 0:16], g3[:, 16:32])
+    g3 = shot_sum()
     bend = bend - mm(nb, mm(g3, b0), 0, 0)
     (b1,) = eliminate((sym(bend), w1))
     es = mm(nb, b1) + stack(b0, jnp.zeros_like(b0))
@@ -388,12 +433,14 @@
         tres_ref[i] = tres[:, i * TB : (i + 1) * TB]
     for w in range(WINS):
         wait_bytes(win.at[w, pl.ds(0, WIN - BR)], hs_sem.at[w])
-    for gm in range(4):
+    for gm in range(3):
         wait_bytes(near.at[gm, pl.ds(0, CELL - 1)], ns_sem.at[gm])
     for gm in range(2):
         wait_bytes(fars[gm].at[pl.ds(0, FAR - 1)], fs_sem.at[gm])
-        wait_bytes(sides[gm].at[pl.ds(0, CELLS - 1)], fs_sem.at[gm + 2])
-        wait_bytes(sides[gm].at[pl.ds(0, 2)], as_sem.at[gm])
+    wait_bytes(side.at[pl.ds(0, CELLS - 1)], fs_sem.at[2])
+    wait_bytes(side.at[pl.ds(0, 2)], as_sem.at[0])
+    wait_bytes(shot.at[pl.ds(0, N_ROW - 1)], fs_sem.at[3])
+    wait_bytes(shot.at[pl.ds(0, len(far_edges))], as_sem.at[1])
 
 
 def per_device(matrix_tiles, column_index, precond, right_side, lost_group):
@@ -415,27 +462,28 @@
             pltpu.VMEM((WIN, 4 * COLS, TB), BF16),
             pltpu.VMEM((WIN, 12 * COLS, TB), BF16),
             pltpu.VMEM((BR, 12 * COLS, K * TB), BF16),
-            pltpu.VMEM((4, 2, COLS, TB), F32),
-            pltpu.VMEM((4, CELL, COLS, TB), F32),
+            pltpu.VMEM((3, 2, COLS, TB), F32),
+            pltpu.VMEM((3, CELL, COLS, TB), F32),
             pltpu.VMEM((FAR, COLS, TB), F32),
             pltpu.VMEM((FAR, COLS, TB), F32),
             pltpu.VMEM((2 * CELLS, COLS, TB), F32),
-            pltpu.VMEM((2 * CELLS, COLS, TB), F32),
+            pltpu.VMEM((2 * N_ROW, COLS // 2, TB), F32),
+            pltpu.VMEM((COLS // 2, TB), F32),
             pltpu.SMEM((BR, K), jnp.int32),
             pltpu.SMEM((1,), jnp.int32),
             pltpu.SMEM((BR, K), jnp.int32),
             dma((4 + BR,)),
             dma((WINS,)),
             dma((WINS,)),
-            dma((4,)),
-            dma((4,)),
+            dma((3,)),
+            dma((3,)),
             dma((4,)),
             dma((4,)),
             dma((2,)),
             dma((2,)),
         ],
         compiler_params=pltpu.CompilerParams(
-            collective_id=0, has_side_effects=True, vmem_limit_bytes=int(64 * 2**20)
+            collective_id=0, has_side_effects=True, vmem_limit_bytes=55136 * 1024
         ),
         name="recover",
     )(column_index, lost_group, matrix_tiles, precond, right_side)

time: 64.9 us -> 59.4 us (0.915)
  Pallas kernels: 60.6 us -> 56 us
  local copies, waits for them, and re-layouts: 2.75 us -> 1.91 us
    pallas_call x1, Pallas kernels: 60.6 us -> 56 us  [per_device(): pl.pallas_call(kernel, out_shape=(shape, shape), in_specs=[hbm, hbm, hbm,...]
    unnamed x2 -> x4, local copies, waits for them, and re-layouts: 2.75 us -> 1.91 us
where the time goes in v3:
time: 59.4 us; the launch traced here: 59.2 us
  Pallas kernels  56 us (94%)
  local copies, waits for them, and re-layouts  1.91 us (3%)
  between operations  1.29 us (2%)
    pallas_call x1, Pallas kernels, per_device(): pl.pallas_call(kernel, out_shape=(shape, shape), in_specs=[hbm, hbm, hbm,...  56 us
    unnamed x4, local copies, waits for them, and re-layouts  1.91 us

profile of v3, /device:TPU:1, one launch (start us, length us, event | category | flops | bytes accessed | tf_op | source)
XLA Modules:
  0.0 59.2 jit_solution(172468757674334504)
XLA Ops:
  1.3 0.0 copy-start
  1.3 0.7 %copy-done = s32[4,32]{1,0:T(4,128)S(1)} copy-done((s32[4,32]{1,0:T(4,128)S(1)}, s32[4,32]{1,0:T(4,128)}, u32[]{:S(2)}) %copy-start) | copy-done | bytes 536
  2.0 56.0 %recover.1 = (f32[4,16,128]{2,1,0:T(8,128)S(1)}, f32[4,16,128]{2,1,0:T(8,128)S(1)}) custom-call(s32[4,32]{1,0:T(4,128)S(1)} %copy-done, s32[1]{0:T(128)S(6)} %copy.9.lost_hbm, f32[4,32,128,128]{3,2,1,0:T(8,128)} %tiles_ref.1, f32[4,128,128]{2,1,0:T(8,128)} %pre_hbm.1, f32[4,16,128]{2,1,0:T(8,128)} %b_hbm.1), custom_call_target="tpu_custom_call" | custom-call | tf_op jit(solution)/shard_map/recover/pallas_call | solution.py:451
  58.0 0.6 %copy.10 = f32[4,16,128]{2,1,0:T(8,128)} copy(f32[4,16,128]{2,1,0:T(8,128)S(1)} %get-tuple-element.4) | data formatting | bytes 65536
  58.6 0.6 %copy.11 = f32[4,16,128]{2,1,0:T(8,128)} copy(f32[4,16,128]{2,1,0:T(8,128)S(1)} %get-tuple-element.5) | data formatting | bytes 65536
Async XLA Ops:
  1.3 0.7 %copy-start = (s32[4,32]{1,0:T(4,128)S(1)}, s32[4,32]{1,0:T(4,128)}, u32[]{:S(2)}) copy-start(s32[4,32]{1,0:T(4,128)} %cols_hbm.1) | copy-start | bytes 1540

commit v4 on v3

--- a/solution.py
+++ b/solution.py
@@ -64,7 +64,7 @@
 
 def kernel(
     cols_hbm, lost_hbm, tiles_ref, pre_hbm, b_hbm, rec_ref, tres_ref,
-    stage, zstage, hl, zhl, win, winb, winc, rhs, msg, near, far0, far1, side, shot, shot_msg, cols_ref, lost_ref, local,
+    stage, zstage, hl, zhl, win, winb, winc, rhs, msg0, msg1, msg2, near0, near1, near2, far0, far1, side, shot, shot_msg, cols_ref, lost_ref, local,
     load_sem, hs_sem, hr_sem, ns_sem, nr_sem, fs_sem, fr_sem, as_sem, ar_sem,
 ):
     g = lax.axis_index("grp")
@@ -90,11 +90,8 @@
     border = jnp.logical_or(r < REACH, r >= N_ROW - REACH)
     offsets = [3, -3, 2, -2, 1, -1]
     fars = [far0, far1]
-
-    for n in range(CELLS):
-        side[CELLS + n] = jnp.zeros((COLS, TB), F32)
-    for n in range(N_ROW):
-        shot[N_ROW + n] = jnp.zeros((COLS // 2, TB), F32)
+    nears = [near0, near1, near2]
+    msgs = [msg0, msg1, msg2]
 
     barrier = pltpu.get_barrier_semaphore()
     for o in offsets:
@@ -132,14 +129,15 @@
         wait_bytes(win.at[w, pl.ds(0, WIN - BR)], hr_sem.at[w])
 
     def near_send(gm, value):
+        msg, near = msgs[gm], nears[gm]
         n_lanes = value.shape[1]
-        value = jnp.concatenate([value, jnp.zeros((COLS, TB - n_lanes), F32)], axis=1)
-        msg[gm, 0] = value
-        near[gm, pos] = value
+        value = jnp.concatenate([value, jnp.zeros((value.shape[0], TB - n_lanes), F32)], axis=1)
+        msg[0] = value
+        near[pos] = value
         for n in range(1, CELL):
             pltpu.make_async_remote_copy(
-                src_ref=msg.at[gm, 0],
-                dst_ref=near.at[gm, pos],
+                src_ref=msg.at[0],
+                dst_ref=near.at[pos],
                 send_sem=ns_sem.at[gm],
                 recv_sem=nr_sem.at[gm],
                 device_id=near_dev(n),
@@ -147,11 +145,12 @@
             ).start()
 
     def near_sum(gm):
-        wait_bytes(near.at[gm, pl.ds(0, CELL - 1)], nr_sem.at[gm])
-        terms = [near[gm, n] for n in range(CELL)]
+        msg, near = msgs[gm], nears[gm]
+        wait_bytes(near.at[pl.ds(0, CELL - 1)], nr_sem.at[gm])
+        terms = [near[n] for n in range(CELL)]
         while len(terms) > 1:
             terms = [terms[n] + terms[n + 1] for n in range(0, len(terms), 2)]
-        msg[gm, 1] = terms[0]
+        msg[1] = terms[0]
         return terms[0]
 
     def far_send(gm):
@@ -159,7 +158,7 @@
         far[my_far] = near_sum(gm)
         for n in range(1, FAR):
             pltpu.make_async_remote_copy(
-                src_ref=msg.at[gm, 1],
+                src_ref=msgs[gm].at[1],
                 dst_ref=far.at[my_far],
                 send_sem=fs_sem.at[gm],
                 recv_sem=fr_sem.at[gm],
@@ -179,7 +178,7 @@
         side[cell] = near_sum(gm)
         for n in range(1, CELLS):
             pltpu.make_async_remote_copy(
-                src_ref=msg.at[gm, 1],
+                src_ref=msgs[gm].at[1],
                 dst_ref=side.at[cell],
                 send_sem=fs_sem.at[gm],
                 recv_sem=fr_sem.at[gm],
@@ -188,7 +187,7 @@
             ).start()
         for step, target in ((1, 0), (N_GRP - 1, CELLS - 1)):
             pltpu.make_async_remote_copy(
-                src_ref=msg.at[gm, 1],
+                src_ref=msgs[gm].at[1],
                 dst_ref=side.at[CELLS + cell],
                 send_sem=as_sem.at[0],
                 recv_sem=ar_sem.at[0],
@@ -211,10 +210,15 @@
 
     far_edges = [(1, 0), (1, 1), (1, 2), (N_GRP - 1, N_ROW - 1), (N_GRP - 1, N_ROW - 2), (N_GRP - 1, N_ROW - 3)]
 
+    def folded(value):
+        half = COLS // 2
+        return jnp.concatenate([value[n * half : (n + 1) * half] for n in range(4)], axis=1)
+
+    def unfolded(value):
+        return jnp.concatenate([value[:, n * COLS : (n + 1) * COLS] for n in range(4)], axis=0)
+
     def shot_send(value):
-        half = COLS // 2
-        parts = [value[n * half : (n + 1) * half] for n in range(4)] + [jnp.zeros((half, TB - 4 * COLS), F32)]
-        value = jnp.concatenate(parts, axis=1)
+        value = jnp.concatenate([folded(value), jnp.zeros((COLS // 2, TB - 4 * COLS), F32)], axis=1)
         shot_msg[...] = value
         shot[r] = value
         for n in range(1, N_ROW):
@@ -249,8 +253,7 @@
             while len(terms) > 1:
                 terms = [terms[n] + terms[n + 1] for n in range(0, len(terms), 2)]
             sums.append(terms[0])
-        total = jnp.where(lost_of[0], sums[1], sums[0])
-        return jnp.concatenate([total[:, n * COLS : (n + 1) * COLS] for n in range(4)], axis=0)
+        return unfolded(jnp.where(lost_of[0], sums[1], sums[0]))
 
     def prepare(w, ref, at):
         for p in range(2 * REACH + 1):
@@ -316,6 +319,11 @@
     (zb,) = condition(v0)
     put(WZ, zb)
     halo_send(WZ)
+    for n in range(CELLS):
+        side[CELLS + n] = jnp.zeros((COLS, TB), F32)
+    for n in range(N_ROW):
+        shot[N_ROW + n] = jnp.zeros((COLS // 2, TB), F32)
+
     loads[2].wait()
 
     def localise(k, carry):
@@ -358,12 +366,11 @@
     halo_wait(WV)
     prepare(WV, winb, 0)
     (own,), (p1,) = product(winb, 1)
+    v2 = own + p1 - v1
+    near_send(1, folded(mm(basis, v2, 1, 1)))
     (zp1,) = condition(p1)
     put(WQ, zp1)
     halo_send(WQ)
-    v2 = own + p1 - v1
-    gb = mm(basis, v2, 1, 1)
-    near_send(1, lanes(gb, (0, 0, 16), (16, 0, 16)))
     one = eye16()
     ga = far_all(0)
     ga = stack(ga[:, 0:32], ga[:, 32:64])
@@ -385,8 +392,7 @@
     prepare(WQ, winc, 8 * COLS)
     (bz, bzp0, bzp1), (oz, ozp0, ozp1) = product(winc, 3)
     y, yp0, yp1 = condition(bz, bzp0, bzp1)
-    gb = far_all(1)
-    gb = stack(gb[:, 0:16], gb[:, 16:32])
+    gb = unfolded(far_all(1))
     curve = curve + mm(dd, mm(gb, d1), 0, 0)
     (a1,) = eliminate((sym(curve), squares))
     cs = mm(dd, a1) + stack(a0, jnp.zeros_like(a0))
@@ -434,7 +440,7 @@
     for w in range(WINS):
         wait_bytes(win.at[w, pl.ds(0, WIN - BR)], hs_sem.at[w])
     for gm in range(3):
-        wait_bytes(near.at[gm, pl.ds(0, CELL - 1)], ns_sem.at[gm])
+        wait_bytes(nears[gm].at[pl.ds(0, CELL - 1)], ns_sem.at[gm])
     for gm in range(2):
         wait_bytes(fars[gm].at[pl.ds(0, FAR - 1)], fs_sem.at[gm])
     wait_bytes(side.at[pl.ds(0, CELLS - 1)], fs_sem.at[2])
@@ -462,10 +468,14 @@
             pltpu.VMEM((WIN, 4 * COLS, TB), BF16),
             pltpu.VMEM((WIN, 12 * COLS, TB), BF16),
             pltpu.VMEM((BR, 12 * COLS, K * TB), BF16),
-            pltpu.VMEM((3, 2, COLS, TB), F32),
-            pltpu.VMEM((3, CELL, COLS, TB), F32),
+            pltpu.VMEM((2, COLS, TB), F32),
+            pltpu.VMEM((2, COLS // 2, TB), F32),
+            pltpu.VMEM((2, COLS, TB), F32),
+            pltpu.VMEM((CELL, COLS, TB), F32),
+            pltpu.VMEM((CELL, COLS // 2, TB), F32),
+            pltpu.VMEM((CELL, COLS, TB), F32),
             pltpu.VMEM((FAR, COLS, TB), F32),
-            pltpu.VMEM((FAR, COLS, TB), F32),
+            pltpu.VMEM((FAR, COLS // 2, TB), F32),
             pltpu.VMEM((2 * CELLS, COLS, TB), F32),
             pltpu.VMEM((2 * N_ROW, COLS // 2, TB), F32),
             pltpu.VMEM((COLS // 2, TB), F32),

time: 59.4 us -> 57.9 us (0.975)
  Pallas kernels: 56 us -> 54.5 us
    pallas_call x1, Pallas kernels: 56 us -> 54.5 us  [per_device(): pl.pallas_call(kernel, out_shape=(shape, shape), in_specs=[hbm, hbm, hbm,...]
where the time goes in v4:
time: 57.9 us; the launch traced here: 57.7 us
  Pallas kernels  54.5 us (94%)
  local copies, waits for them, and re-layouts  1.91 us (3%)
  between operations  1.29 us (2%)
    pallas_call x1, Pallas kernels, per_device(): pl.pallas_call(kernel, out_shape=(shape, shape), in_specs=[hbm, hbm, hbm,...  54.5 us
    unnamed x4, local copies, waits for them, and re-layouts  1.91 us

profile of v4, /device:TPU:1, one launch (start us, length us, event | category | flops | bytes accessed | tf_op | source)
XLA Modules:
  0.0 57.7 jit_solution(3183709600752128401)
XLA Ops:
  1.3 0.0 copy-start
  1.3 0.7 %copy-done = s32[4,32]{1,0:T(4,128)S(1)} copy-done((s32[4,32]{1,0:T(4,128)S(1)}, s32[4,32]{1,0:T(4,128)}, u32[]{:S(2)}) %copy-start) | copy-done | bytes 536
  2.0 54.5 %recover.1 = (f32[4,16,128]{2,1,0:T(8,128)S(1)}, f32[4,16,128]{2,1,0:T(8,128)S(1)}) custom-call(s32[4,32]{1,0:T(4,128)S(1)} %copy-done, s32[1]{0:T(128)S(6)} %copy.9.lost_hbm, f32[4,32,128,128]{3,2,1,0:T(8,128)} %tiles_ref.1, f32[4,128,128]{2,1,0:T(8,128)} %pre_hbm.1, f32[4,16,128]{2,1,0:T(8,128)} %b_hbm.1), custom_call_target="tpu_custom_call" | custom-call | tf_op jit(solution)/shard_map/recover/pallas_call | solution.py:457
  56.5 0.6 %copy.10 = f32[4,16,128]{2,1,0:T(8,128)} copy(f32[4,16,128]{2,1,0:T(8,128)S(1)} %get-tuple-element.4) | data formatting | bytes 65536
  57.1 0.6 %copy.11 = f32[4,16,128]{2,1,0:T(8,128)} copy(f32[4,16,128]{2,1,0:T(8,128)S(1)} %get-tuple-element.5) | data formatting | bytes 65536
Async XLA Ops:
  1.3 0.7 %copy-start = (s32[4,32]{1,0:T(4,128)S(1)}, s32[4,32]{1,0:T(4,128)}, u32[]{:S(2)}) copy-start(s32[4,32]{1,0:T(4,128)} %cols_hbm.1) | copy-start | bytes 1540

commit v5 on v4

--- a/solution.py
+++ b/solution.py
@@ -19,6 +19,20 @@
 CELLS = N_ROW // CELL
 WB, WZ, WV, WP, WQ, WT = range(6)
 WINS = 6
+
+
+def farthest_first(steps):
+    def hops(step):
+        return -sum(min(n, size - n) * weight for n, size, weight in zip(step, *steps[1:]))
+
+    return sorted(steps[0], key=hops)
+
+
+NEAR_STEPS = farthest_first(([(z, c) for z in range(4) for c in range(2) if z + c], (4, 2), (2, 1)))
+FAR_STEPS = farthest_first(([(x, y) for x in range(4) for y in range(4) if x + y], (4, 4), (1, 1)))
+SHOT_STEPS = farthest_first(
+    ([(y, z, c) for y in range(4) for z in range(4) for c in range(2) if y + z + c], (4, 4, 2), (2, 2, 1))
+)
 
 
 def mm(a, b, ca=1, cb=0):
@@ -76,12 +90,17 @@
     first = d * BR - BAND
     total_devices = N_GRP * N_ROW
 
-    def near_dev(n):
-        return (g, cell * CELL + lax.rem(pos + n, CELL))
-
-    def far_dev(n):
-        f = lax.rem(my_far + n, FAR)
-        return (f // CELLS, lax.rem(f, CELLS) * CELL + pos)
+    def place(step_z, step_c):
+        return lax.rem(pos // 2 + step_z, CELL // 2) * 2 + lax.rem(pos + step_c, 2)
+
+    def near_dev(step):
+        return (g, cell * CELL + place(*step))
+
+    def far_dev(step):
+        return (lax.rem(g + step[0], N_GRP), lax.rem(cell + step[1], CELLS) * CELL + pos)
+
+    def shot_dev(step):
+        return (g, lax.rem(cell + step[0], CELLS) * CELL + place(*step[1:]))
 
     def halo_dev(o):
         t = lax.rem(d + o + total_devices, total_devices)
@@ -96,9 +115,9 @@
     barrier = pltpu.get_barrier_semaphore()
     for o in offsets:
         pl.semaphore_signal(barrier, inc=1, device_id=halo_dev(o), device_id_type=MESH)
-    for n in range(1, FAR):
+    for n in FAR_STEPS:
         pl.semaphore_signal(barrier, inc=1, device_id=far_dev(n), device_id_type=MESH)
-    for n in range(1, CELL):
+    for n in NEAR_STEPS:
         pl.semaphore_signal(barrier, inc=1, device_id=near_dev(n), device_id_type=MESH)
 
     own_span = pl.ds(BAND, BR)
@@ -134,7 +153,7 @@
         value = jnp.concatenate([value, jnp.zeros((value.shape[0], TB - n_lanes), F32)], axis=1)
         msg[0] = value
         near[pos] = value
-        for n in range(1, CELL):
+        for n in NEAR_STEPS:
             pltpu.make_async_remote_copy(
                 src_ref=msg.at[0],
                 dst_ref=near.at[pos],
@@ -156,7 +175,7 @@
     def far_send(gm):
         far = fars[gm]
         far[my_far] = near_sum(gm)
-        for n in range(1, FAR):
+        for n in FAR_STEPS:
             pltpu.make_async_remote_copy(
                 src_ref=msgs[gm].at[1],
                 dst_ref=far.at[my_far],
@@ -176,7 +195,7 @@
 
     def side_send(gm):
         side[cell] = near_sum(gm)
-        for n in range(1, CELLS):
+        for n in (2, 1, 3):
             pltpu.make_async_remote_copy(
                 src_ref=msgs[gm].at[1],
                 dst_ref=side.at[cell],
@@ -221,15 +240,6 @@
         value = jnp.concatenate([folded(value), jnp.zeros((COLS // 2, TB - 4 * COLS), F32)], axis=1)
         shot_msg[...] = value
         shot[r] = value
-        for n in range(1, N_ROW):
-            pltpu.make_async_remote_copy(
-                src_ref=shot_msg,
-                dst_ref=shot.at[r],
-                send_sem=fs_sem.at[3],
-                recv_sem=fr_sem.at[3],
-                device_id=(g, lax.rem(r + n, N_ROW)),
-                device_id_type=MESH,
-            ).start()
         for step, target in far_edges:
             pltpu.make_async_remote_copy(
                 src_ref=shot_msg,
@@ -237,6 +247,15 @@
                 send_sem=as_sem.at[1],
                 recv_sem=ar_sem.at[1],
                 device_id=(lax.rem(g + step, N_GRP), target),
+                device_id_type=MESH,
+            ).start()
+        for n in SHOT_STEPS:
+            pltpu.make_async_remote_copy(
+                src_ref=shot_msg,
+                dst_ref=shot.at[r],
+                send_sem=fs_sem.at[3],
+                recv_sem=fr_sem.at[3],
+                device_id=shot_dev(n),
                 device_id_type=MESH,
             ).start()
 

time: 57.9 us -> 57.7 us (level)
  no operation moved by 1% of the time
where the time goes in v5:
time: 57.7 us; the launch traced here: 57.6 us
  Pallas kernels  54.4 us (94%)
  local copies, waits for them, and re-layouts  1.91 us (3%)
  between operations  1.29 us (2%)
    pallas_call x1, Pallas kernels, per_device(): pl.pallas_call(kernel, out_shape=(shape, shape), in_specs=[hbm, hbm, hbm,...  54.4 us
    unnamed x4, local copies, waits for them, and re-layouts  1.91 us

profile of v5, /device:TPU:1, one launch (start us, length us, event | category | flops | bytes accessed | tf_op | source)
XLA Modules:
  0.0 57.6 jit_solution(3351297696374218193)
XLA Ops:
  1.3 0.0 copy-start
  1.3 0.7 %copy-done = s32[4,32]{1,0:T(4,128)S(1)} copy-done((s32[4,32]{1,0:T(4,128)S(1)}, s32[4,32]{1,0:T(4,128)}, u32[]{:S(2)}) %copy-start) | copy-done | bytes 536
  2.0 54.4 %recover.1 = (f32[4,16,128]{2,1,0:T(8,128)S(1)}, f32[4,16,128]{2,1,0:T(8,128)S(1)}) custom-call(s32[4,32]{1,0:T(4,128)S(1)} %copy-done, s32[1]{0:T(128)S(6)} %copy.9.lost_hbm, f32[4,32,128,128]{3,2,1,0:T(8,128)} %tiles_ref.1, f32[4,128,128]{2,1,0:T(8,128)} %pre_hbm.1, f32[4,16,128]{2,1,0:T(8,128)} %b_hbm.1), custom_call_target="tpu_custom_call" | custom-call | tf_op jit(solution)/shard_map/recover/pallas_call | solution.py:476
  56.3 0.6 %copy.10 = f32[4,16,128]{2,1,0:T(8,128)} copy(f32[4,16,128]{2,1,0:T(8,128)S(1)} %get-tuple-element.4) | data formatting | bytes 65536
  56.9 0.6 %copy.11 = f32[4,16,128]{2,1,0:T(8,128)} copy(f32[4,16,128]{2,1,0:T(8,128)S(1)} %get-tuple-element.5) | data formatting | bytes 65536
Async XLA Ops:
  1.3 0.7 %copy-start = (s32[4,32]{1,0:T(4,128)S(1)}, s32[4,32]{1,0:T(4,128)}, u32[]{:S(2)}) copy-start(s32[4,32]{1,0:T(4,128)} %cols_hbm.1) | copy-start | bytes 1540

commit v6 on v5

--- a/solution.py
+++ b/solution.py
@@ -133,11 +133,11 @@
     def wait_bytes(ref, sem):
         pltpu.make_async_copy(ref, ref, sem).wait()
 
-    def halo_send(w):
+    def halo_send(w, start=0, count=BR):
         for o in offsets:
             pltpu.make_async_remote_copy(
-                src_ref=win.at[w, own_span],
-                dst_ref=win.at[w, pl.ds((REACH - o) * BR, BR)],
+                src_ref=win.at[w, pl.ds(BAND + start, count)],
+                dst_ref=win.at[w, pl.ds((REACH - o) * BR + start, count)],
                 send_sem=hs_sem.at[w],
                 recv_sem=hr_sem.at[w],
                 device_id=halo_dev(o),
@@ -286,7 +286,7 @@
                     [hi_own, lo_own, hi - hi_own, lo - lo_own], axis=0
                 )
 
-    def product(ref, count):
+    def product(ref, count, after=None):
         own = [[] for _ in range(count)]
         other = [[] for _ in range(count)]
         rows = 4 * COLS * count
@@ -300,6 +300,8 @@
                 other[n].append(
                     o[(4 * n + 2) * COLS : (4 * n + 3) * COLS] + o[(4 * n + 3) * COLS : (4 * n + 4) * COLS]
                 )
+            if after is not None:
+                after(i, own[0][i], other[0][i])
         return [jnp.concatenate(v, axis=1) for v in own], [jnp.concatenate(v, axis=1) for v in other]
 
     def condition(*vectors):
@@ -337,7 +339,6 @@
     v0 = jnp.concatenate([win[WB, BAND + i] for i in range(BR)], axis=1)
     (zb,) = condition(v0)
     put(WZ, zb)
-    halo_send(WZ)
     for n in range(CELLS):
         side[CELLS + n] = jnp.zeros((COLS, TB), F32)
     for n in range(N_ROW):
@@ -363,14 +364,18 @@
 
         lax.fori_loop(0, K, convert, 0)
     halo_wait(WB)
+    halo_send(WZ)
     prepare(WB, winb, 0)
-    (own,), (p0,) = product(winb, 1)
+
+    def send_rows(i, own, other):
+        win[WV, BAND + i] = own + other - v0[:, i * TB : (i + 1) * TB]
+        if i % 2 == 1:
+            halo_send(WV, i - 1, 2)
+
+    (own,), (p0,) = product(winb, 1, send_rows)
     v1 = own + p0 - v0
-    put(WV, v1)
-    halo_send(WV)
     (zp0,) = condition(p0)
     put(WP, zp0)
-    halo_send(WP)
     basis = stack(v0, v1)
     ga = mm(basis, basis, 1, 1)
     near_send(0, lanes(ga, (0, 0, 32), (16, 0, 32)))
@@ -383,6 +388,7 @@
     prepare(WZ, winc, 0)
     far_send(0)
     halo_wait(WV)
+    halo_send(WP)
     prepare(WV, winb, 0)
     (own,), (p1,) = product(winb, 1)
     v2 = own + p1 - v1

time: 57.7 us -> 56.2 us (0.974)
  Pallas kernels: 54.4 us -> 52.9 us
    pallas_call x1, Pallas kernels: 54.4 us -> 52.9 us  [per_device(): pl.pallas_call(kernel, out_shape=(shape, shape), in_specs=[hbm, hbm, hbm,...]
where the time goes in v6:
time: 56.2 us; the launch traced here: 56.1 us
  Pallas kernels  52.9 us (94%)
  local copies, waits for them, and re-layouts  1.91 us (3%)
  between operations  1.29 us (2%)
    pallas_call x1, Pallas kernels, per_device(): pl.pallas_call(kernel, out_shape=(shape, shape), in_specs=[hbm, hbm, hbm,...  52.9 us
    unnamed x4, local copies, waits for them, and re-layouts  1.91 us

profile of v6, /device:TPU:1, one launch (start us, length us, event | category | flops | bytes accessed | tf_op | source)
XLA Modules:
  0.0 56.1 jit_solution(10441277896068685165)
XLA Ops:
  1.3 0.0 copy-start
  1.3 0.7 %copy-done = s32[4,32]{1,0:T(4,128)S(1)} copy-done((s32[4,32]{1,0:T(4,128)S(1)}, s32[4,32]{1,0:T(4,128)}, u32[]{:S(2)}) %copy-start) | copy-done | bytes 536
  2.0 52.9 %recover.1 = (f32[4,16,128]{2,1,0:T(8,128)S(1)}, f32[4,16,128]{2,1,0:T(8,128)S(1)}) custom-call(s32[4,32]{1,0:T(4,128)S(1)} %copy-done, s32[1]{0:T(128)S(6)} %copy.9.lost_hbm, f32[4,32,128,128]{3,2,1,0:T(8,128)} %tiles_ref.1, f32[4,128,128]{2,1,0:T(8,128)} %pre_hbm.1, f32[4,16,128]{2,1,0:T(8,128)} %b_hbm.1), custom_call_target="tpu_custom_call" | custom-call | tf_op jit(solution)/shard_map/recover/pallas_call | solution.py:482
  54.8 0.6 %copy.10 = f32[4,16,128]{2,1,0:T(8,128)} copy(f32[4,16,128]{2,1,0:T(8,128)S(1)} %get-tuple-element.4) | data formatting | bytes 65536
  55.4 0.6 %copy.11 = f32[4,16,128]{2,1,0:T(8,128)} copy(f32[4,16,128]{2,1,0:T(8,128)S(1)} %get-tuple-element.5) | data formatting | bytes 65536
Async XLA Ops:
  1.3 0.7 %copy-start = (s32[4,32]{1,0:T(4,128)S(1)}, s32[4,32]{1,0:T(4,128)}, u32[]{:S(2)}) copy-start(s32[4,32]{1,0:T(4,128)} %cols_hbm.1) | copy-start | bytes 1540

commit v7 on v6

--- a/solution.py
+++ b/solution.py
@@ -369,8 +369,7 @@
 
     def send_rows(i, own, other):
         win[WV, BAND + i] = own + other - v0[:, i * TB : (i + 1) * TB]
-        if i % 2 == 1:
-            halo_send(WV, i - 1, 2)
+        halo_send(WV, i, 1)
 
     (own,), (p0,) = product(winb, 1, send_rows)
     v1 = own + p0 - v0

time: 56.2 us -> 58.5 us (1.041)
  Pallas kernels: 52.9 us -> 55.2 us
    pallas_call x1, Pallas kernels: 52.9 us -> 55.2 us  [per_device(): pl.pallas_call(kernel, out_shape=(shape, shape), in_specs=[hbm, hbm, hbm,...]
where the time goes in v7:
time: 58.5 us; the launch traced here: 58.4 us
  Pallas kernels  55.2 us (94%)
  local copies, waits for them, and re-layouts  1.91 us (3%)
  between operations  1.29 us (2%)
    pallas_call x1, Pallas kernels, per_device(): pl.pallas_call(kernel, out_shape=(shape, shape), in_specs=[hbm, hbm, hbm,...  55.2 us
    unnamed x4, local copies, waits for them, and re-layouts  1.91 us

profile of v7, /device:TPU:1, one launch (start us, length us, event | category | flops | bytes accessed | tf_op | source)
XLA Modules:
  0.0 58.4 jit_solution(14718609921630510470)
XLA Ops:
  1.3 0.0 copy-start
  1.3 0.7 %copy-done = s32[4,32]{1,0:T(4,128)S(1)} copy-done((s32[4,32]{1,0:T(4,128)S(1)}, s32[4,32]{1,0:T(4,128)}, u32[]{:S(2)}) %copy-start) | copy-done | bytes 536
  2.0 55.2 %recover.1 = (f32[4,16,128]{2,1,0:T(8,128)S(1)}, f32[4,16,128]{2,1,0:T(8,128)S(1)}) custom-call(s32[4,32]{1,0:T(4,128)S(1)} %copy-done, s32[1]{0:T(128)S(6)} %copy.9.lost_hbm, f32[4,32,128,128]{3,2,1,0:T(8,128)} %tiles_ref.1, f32[4,128,128]{2,1,0:T(8,128)} %pre_hbm.1, f32[4,16,128]{2,1,0:T(8,128)} %b_hbm.1), custom_call_target="tpu_custom_call" | custom-call | tf_op jit(solution)/shard_map/recover/pallas_call | solution.py:481
  57.1 0.6 %copy.10 = f32[4,16,128]{2,1,0:T(8,128)} copy(f32[4,16,128]{2,1,0:T(8,128)S(1)} %get-tuple-element.4) | data formatting | bytes 65536
  57.8 0.6 %copy.11 = f32[4,16,128]{2,1,0:T(8,128)} copy(f32[4,16,128]{2,1,0:T(8,128)S(1)} %get-tuple-element.5) | data formatting | bytes 65536
Async XLA Ops:
  1.3 0.7 %copy-start = (s32[4,32]{1,0:T(4,128)S(1)}, s32[4,32]{1,0:T(4,128)}, u32[]{:S(2)}) copy-start(s32[4,32]{1,0:T(4,128)} %cols_hbm.1) | copy-start | bytes 1540
